TPU v7x, 32 devices: a whole 2x2x4 slice. The times are simulated.
32 devices in a mesh: batch: 16 (over z, y, core), seq: 2 (over x).
Axes of the slice: x: 2, y: 2, z: 4, core: 2. Of those that a mesh axis runs over, the one named last changes fastest.
Arguments:
- tables_in: bfloat16 [64, 512, 768], P('batch', 'seq'), may hold values from -6 to 6
- out_cot: bfloat16 [64, 512, 768], P('batch', 'seq'), may hold values from -6 to 6
- segment_ids: int32 [64, 512], P('batch'), may hold values from 0 to 1, as said below
- row_ids: int32 [64, 512], P('batch'), may hold values from 0 to 15
- col_ids: int32 [64, 512], P('batch'), may hold values from 0 to 11
- qkv_weight: bfloat16 [3, 768, 768], replicated, may hold values from -0.21875 to 0.21875
- out_weight: bfloat16 [768, 768], replicated, may hold values from -2.5 to 2.5
- ffn_in_weight: bfloat16 [768, 3072], replicated, may hold values from -0.21875 to 0.21875
- ffn_out_weight: bfloat16 [3072, 768], replicated, may hold values from -0.109375 to 0.109375
- small_params: float32 [9216], replicated
- qkv_master: float32 [3, 768, 768], P(None, ('batch', 'seq')), may hold values from -0.21875 to 0.21875
- qkv_first: float32 [3, 768, 768], P(None, ('batch', 'seq')), may hold values from -0.66 to 0.66
- qkv_second: float32 [3, 768, 768], P(None, ('batch', 'seq')), may hold values from 0.001 to 0.004
- qkv_ema: float32 [3, 768, 768], P(None, ('batch', 'seq')), may hold values from -0.21875 to 0.21875
- out_master: float32 [768, 768], P(('batch', 'seq')), may hold values from -2.5 to 2.5
- out_first: float32 [768, 768], P(('batch', 'seq')), may hold values from -0.66 to 0.66
- out_second: float32 [768, 768], P(('batch', 'seq')), may hold values from 0.00025 to 0.001
- out_ema: float32 [768, 768], P(('batch', 'seq')), may hold values from -2.5 to 2.5
- ffn_in_master: float32 [768, 3072], P(('batch', 'seq')), may hold values from -0.21875 to 0.21875
- ffn_in_first: float32 [768, 3072], P(('batch', 'seq')), may hold values from -0.66 to 0.66
- ffn_in_second: float32 [768, 3072], P(('batch', 'seq')), may hold values from 0.001 to 0.004
- ffn_in_ema: float32 [768, 3072], P(('batch', 'seq')), may hold values from -0.21875 to 0.21875
- ffn_out_master: float32 [3072, 768], P(('batch', 'seq')), may hold values from -0.109375 to 0.109375
- ffn_out_first: float32 [3072, 768], P(('batch', 'seq')), may hold values from -0.66 to 0.66
- ffn_out_second: float32 [3072, 768], P(('batch', 'seq')), may hold values from 0.001 to 0.004
- ffn_out_ema: float32 [3072, 768], P(('batch', 'seq')), may hold values from -0.109375 to 0.109375
- small_first: float32 [9216], replicated, may hold values from -1.2 to 1.2
- small_second: float32 [9216], replicated, may hold values from 0.002 to 0.03
- small_ema: float32 [9216], replicated
Outputs:
- layer_out: bfloat16 [64, 512, 768], P('batch', 'seq')
- input_grad: bfloat16 [64, 512, 768], P('batch', 'seq')
- qkv_grad: float32 [3, 768, 768], P(None, ('batch', 'seq'))
- out_grad: float32 [768, 768], P(('batch', 'seq'))
- ffn_in_grad: float32 [768, 3072], P(('batch', 'seq'))
- ffn_out_grad: float32 [3072, 768], P(('batch', 'seq'))
- small_grad: float32 [9216], replicated
- grad_norm: float32 [], replicated
- qkv_first_new: float32 [3, 768, 768], P(None, ('batch', 'seq'))
- qkv_second_new: float32 [3, 768, 768], P(None, ('batch', 'seq'))
- qkv_master_new: float32 [3, 768, 768], P(None, ('batch', 'seq'))
- qkv_copy_new: bfloat16 [3, 768, 768], P(None, ('batch', 'seq'))
- qkv_ema_new: float32 [3, 768, 768], P(None, ('batch', 'seq'))
- out_first_new: float32 [768, 768], P(('batch', 'seq'))
- out_second_new: float32 [768, 768], P(('batch', 'seq'))
- out_master_new: float32 [768, 768], P(('batch', 'seq'))
- out_copy_new: bfloat16 [768, 768], P(('batch', 'seq'))
- out_ema_new: float32 [768, 768], P(('batch', 'seq'))
- ffn_in_first_new: float32 [768, 3072], P(('batch', 'seq'))
- ffn_in_second_new: float32 [768, 3072], P(('batch', 'seq'))
- ffn_in_master_new: float32 [768, 3072], P(('batch', 'seq'))
- ffn_in_copy_new: bfloat16 [768, 3072], P(('batch', 'seq'))
- ffn_in_ema_new: float32 [768, 3072], P(('batch', 'seq'))
- ffn_out_first_new: float32 [3072, 768], P(('batch', 'seq'))
- ffn_out_second_new: float32 [3072, 768], P(('batch', 'seq'))
- ffn_out_master_new: float32 [3072, 768], P(('batch', 'seq'))
- ffn_out_copy_new: bfloat16 [3072, 768], P(('batch', 'seq'))
- ffn_out_ema_new: float32 [3072, 768], P(('batch', 'seq'))
- small_first_new: float32 [9216], replicated
- small_second_new: float32 [9216], replicated
- small_new: float32 [9216], replicated
- small_ema_new: float32 [9216], replicated
Inputs may be any that keep to these rules, and one draw needn't show every extreme that they name: In each table, segment_ids are 0 on the first n tokens and 1 on the rest, with 32 <= n <= 128.
All inputs are finite; a program needn't handle non-finite values.
Results may differ from a plain program's by a relative error of at most 0.015.
Values may be sent and summed in bfloat16 or wider, within the bound.
A program may use at most 192 MiB of HBM per device.

v0:
```python
import math

import jax
import jax.numpy as jnp
from jax import lax
from jax.sharding import PartitionSpec as P

HD = 64
STEP = 10


EPS_NORM = 1e-06
NEG_BIG = -1e30
BETA_ONE = 0.9
BETA_TWO = 0.999
ADAM_EPS = 1e-08
DECAY = 0.01
EMA_KEEP = 0.8
SMALL_RATE = 0.1


def norm_rows(rows, gain, shift):
    centre = rows - jnp.mean(rows, axis=-1, keepdims=True)
    spread = jnp.mean(centre * centre, axis=-1, keepdims=True)
    return centre * lax.rsqrt(spread + EPS_NORM) * gain + shift


def gelu_exact(values):
    return jax.nn.gelu(values, approximate=False)


def split_small(small_terms, model_width, hidden_units):
    pieces = [small_terms[offset * model_width : (offset + 1) * model_width] for offset in range(8)]
    return pieces + [small_terms[8 * model_width : 8 * model_width + hidden_units]]


def visible_pair(seg_query, row_query, col_query, seg_key, row_key, col_key):
    return (
        (seg_query[..., :, None] == 0)
        | (seg_key[..., None, :] == 0)
        | (row_query[..., :, None] == row_key[..., None, :])
        | (col_query[..., :, None] == col_key[..., None, :])
    )


def product(left, right):
    return jnp.dot(left, right, preferred_element_type=jnp.float32)


def product_left_t(left, right):
    return lax.dot_general(
        left, right, (((0,), (0,)), ((), ())), preferred_element_type=jnp.float32
    )


def product_right_t(left, right):
    return lax.dot_general(
        left, right, (((1,), (1,)), ((), ())), preferred_element_type=jnp.float32
    )


def adam_update(grad_new, first, second, master, ema_old, rate):
    first_new = BETA_ONE * first + (1.0 - BETA_ONE) * grad_new
    second_new = BETA_TWO * second + (1.0 - BETA_TWO) * grad_new * grad_new
    fix_one = 1.0 - BETA_ONE**STEP
    fix_two = 1.0 - BETA_TWO**STEP
    master_new = master - rate * (
        first_new / fix_one / (jnp.sqrt(second_new / fix_two) + ADAM_EPS) + DECAY * master
    )
    ema_new = EMA_KEEP * ema_old + (1.0 - EMA_KEEP) * master_new
    return (first_new, second_new, master_new, ema_new)


def body(
    tables_in,
    out_cot,
    segment_ids,
    row_ids,
    col_ids,
    qkv_weight,
    out_weight,
    ffn_in_weight,
    ffn_out_weight,
    small_params,
    qkv_master,
    qkv_first,
    qkv_second,
    qkv_ema,
    out_master,
    out_first,
    out_second,
    out_ema,
    ffn_in_master,
    ffn_in_first,
    ffn_in_second,
    ffn_in_ema,
    ffn_out_master,
    ffn_out_first,
    ffn_out_second,
    ffn_out_ema,
    small_first,
    small_second,
    small_ema,
):
    model_width = qkv_weight.shape[1]
    hidden_units = ffn_in_weight.shape[1]
    heads = model_width // HD
    head_scale = HD ** (-0.5)
    seq_place = lax.axis_index("seq")
    local_x, local_cot = (tables_in, out_cot)
    tab_count = local_x.shape[0]
    block_rows = local_x.shape[1]
    seg_keys, row_keys, col_keys = (segment_ids, row_ids, col_ids)
    seg_query = lax.dynamic_slice_in_dim(segment_ids, seq_place * block_rows, block_rows, 1)
    row_query = lax.dynamic_slice_in_dim(row_ids, seq_place * block_rows, block_rows, 1)
    col_query = lax.dynamic_slice_in_dim(col_ids, seq_place * block_rows, block_rows, 1)
    row_count = tab_count * block_rows
    (
        gain_one,
        gain_two,
        shift_one,
        shift_two,
        bias_query,
        bias_value,
        bias_attn,
        bias_ffn,
        bias_inner,
    ) = split_small(small_params, model_width, hidden_units)
    flat_x = local_x.reshape(row_count, model_width)
    query_low = (product(flat_x, qkv_weight[0]) + bias_query).astype(jnp.bfloat16)
    key_low = (
        product(flat_x, qkv_weight[1])
        .astype(jnp.bfloat16)
        .reshape(tab_count, block_rows, model_width)
    )
    value_low = (
        (product(flat_x, qkv_weight[2]) + bias_value)
        .astype(jnp.bfloat16)
        .reshape(tab_count, block_rows, model_width)
    )
    key_all, value_all = (
        lax.all_gather(key_low, "seq", axis=1, tiled=True),
        lax.all_gather(value_low, "seq", axis=1, tiled=True),
    )
    rows_key = key_all.shape[1]
    query_heads = query_low.reshape(tab_count, block_rows, heads, HD)
    key_heads = key_all.reshape(tab_count, rows_key, heads, HD)
    value_heads = value_all.reshape(tab_count, rows_key, heads, HD)
    allowed = visible_pair(seg_query, row_query, col_query, seg_keys, row_keys, col_keys)[:, None]

    def scores_of():
        raw = (
            jnp.einsum(
                "bqhe,bkhe->bhqk", query_heads, key_heads, preferred_element_type=jnp.float32
            )
            * head_scale
        )
        return jnp.where(allowed, raw, NEG_BIG)

    scores = scores_of()
    top_score = jnp.max(scores, axis=-1, keepdims=True)
    exp_scores = jnp.exp(scores - top_score)
    exp_total = jnp.sum(exp_scores, axis=-1, keepdims=True)
    log_total = top_score + jnp.log(exp_total)
    prob_low = (exp_scores / exp_total).astype(jnp.bfloat16)
    context = jnp.einsum(
        "bhqk,bkhe->bqhe", prob_low, value_heads, preferred_element_type=jnp.float32
    )
    context_low = context.astype(jnp.bfloat16).reshape(row_count, model_width)
    attn = product(context_low, out_weight) + bias_attn
    first_sum = flat_x.astype(jnp.float32) + attn
    normed, first_back = jax.vjp(norm_rows, first_sum, gain_one, shift_one)
    normed_low = normed.astype(jnp.bfloat16)
    ffn_inner = product(normed_low, ffn_in_weight) + bias_inner
    active, gelu_back = jax.vjp(gelu_exact, ffn_inner)
    active_low = active.astype(jnp.bfloat16)
    branch = product(active_low, ffn_out_weight) + bias_ffn
    second_sum = normed + branch
    result, second_back = jax.vjp(norm_rows, second_sum, gain_two, shift_two)
    layer_out = result.astype(jnp.bfloat16).reshape(tab_count, block_rows, model_width)
    back_rows = local_cot.reshape(row_count, model_width).astype(jnp.float32)
    d_second, d_gain_two, d_shift_two = second_back(back_rows)
    d_branch = d_second.astype(jnp.bfloat16)
    d_bias_ffn = jnp.sum(d_branch.astype(jnp.float32), axis=0)
    g_outer = product_left_t(active_low, d_branch)
    d_active = product_right_t(d_branch, ffn_out_weight)
    (d_inner,) = gelu_back(d_active)
    d_inner_low = d_inner.astype(jnp.bfloat16)
    d_bias_inner = jnp.sum(d_inner_low.astype(jnp.float32), axis=0)
    g_inner = product_left_t(normed_low, d_inner_low)
    d_normed = product_right_t(d_inner_low, ffn_in_weight) + d_second
    d_first, d_gain_one, d_shift_one = first_back(d_normed)
    d_attn = d_first.astype(jnp.bfloat16)
    d_bias_attn = jnp.sum(d_attn.astype(jnp.float32), axis=0)
    g_attn = product_left_t(context_low, d_attn)
    d_context = (
        product_right_t(d_attn, out_weight)
        .astype(jnp.bfloat16)
        .reshape(tab_count, block_rows, heads, HD)
    )
    probs_again = jnp.exp(scores_of() - log_total)
    probs_again_low = probs_again.astype(jnp.bfloat16)
    d_value = jnp.einsum(
        "bhqk,bqhe->bkhe", probs_again_low, d_context, preferred_element_type=jnp.float32
    )
    d_probs = jnp.einsum(
        "bqhe,bkhe->bhqk", d_context, value_heads, preferred_element_type=jnp.float32
    )
    d_scores = probs_again * (d_probs - jnp.sum(d_probs * probs_again, axis=-1, keepdims=True))
    d_scores_low = d_scores.astype(jnp.bfloat16)
    d_query = (
        jnp.einsum("bhqk,bkhe->bqhe", d_scores_low, key_heads, preferred_element_type=jnp.float32)
        * head_scale
    )
    d_key = (
        jnp.einsum("bhqk,bqhe->bkhe", d_scores_low, query_heads, preferred_element_type=jnp.float32)
        * head_scale
    )
    d_key, d_value = (
        lax.psum_scatter(d_key.astype(jnp.bfloat16), "seq", scatter_dimension=1, tiled=True).astype(
            jnp.float32
        ),
        lax.psum_scatter(
            d_value.astype(jnp.bfloat16), "seq", scatter_dimension=1, tiled=True
        ).astype(jnp.float32),
    )
    d_query_low = d_query.astype(jnp.bfloat16).reshape(row_count, model_width)
    d_key_low = d_key.astype(jnp.bfloat16).reshape(row_count, model_width)
    d_value_low = d_value.astype(jnp.bfloat16).reshape(row_count, model_width)
    d_bias_query = jnp.sum(d_query_low.astype(jnp.float32), axis=0)
    d_bias_value = jnp.sum(d_value_low.astype(jnp.float32), axis=0)
    g_qkv = jnp.stack(
        [
            product_left_t(flat_x, d_query_low),
            product_left_t(flat_x, d_key_low),
            product_left_t(flat_x, d_value_low),
        ]
    )
    d_input = (
        d_first
        + product_right_t(d_query_low, qkv_weight[0])
        + product_right_t(d_key_low, qkv_weight[1])
        + product_right_t(d_value_low, qkv_weight[2])
    )
    input_grad = d_input.astype(jnp.bfloat16).reshape(tab_count, block_rows, model_width)
    small_terms = jnp.concatenate(
        [
            d_gain_one,
            d_gain_two,
            d_shift_one,
            d_shift_two,
            d_bias_query,
            d_bias_value,
            d_bias_attn,
            d_bias_ffn,
            d_bias_inner,
        ]
    )
    full_qkv, full_attn, full_inner, full_outer, small_sum = lax.psum(
        (g_qkv, g_attn, g_inner, g_outer, small_terms), ("batch", "seq")
    )
    total_sq = (
        jnp.sum(full_qkv * full_qkv)
        + jnp.sum(full_attn * full_attn)
        + jnp.sum(full_inner * full_inner)
        + jnp.sum(full_outer * full_outer)
        + jnp.sum(small_sum * small_sum)
    )
    shard_index = lax.axis_index(("batch", "seq"))
    share_qkv = lax.dynamic_slice_in_dim(
        full_qkv, shard_index * qkv_master.shape[1], qkv_master.shape[1], 1
    )
    share_attn = lax.dynamic_slice_in_dim(
        full_attn, shard_index * out_master.shape[0], out_master.shape[0], 0
    )
    share_inner = lax.dynamic_slice_in_dim(
        full_inner, shard_index * ffn_in_master.shape[0], ffn_in_master.shape[0], 0
    )
    share_outer = lax.dynamic_slice_in_dim(
        full_outer, shard_index * ffn_out_master.shape[0], ffn_out_master.shape[0], 0
    )
    grad_norm = jnp.sqrt(total_sq)
    clip_limit = math.sqrt(
        float(
            4 * model_width * model_width
            + 2 * model_width * hidden_units
            + 8 * model_width
            + hidden_units
        )
    )
    clip_scale = jnp.minimum(1.0, clip_limit / grad_norm)
    qkv_grad = share_qkv * clip_scale
    out_grad = share_attn * clip_scale
    ffn_in_grad = share_inner * clip_scale
    ffn_out_grad = share_outer * clip_scale
    small_grad = small_sum * clip_scale
    qf, qs, qm, qe = adam_update(
        qkv_grad, qkv_first, qkv_second, qkv_master, qkv_ema, model_width ** (-0.5)
    )
    of, osec, om, oe = adam_update(
        out_grad, out_first, out_second, out_master, out_ema, max(model_width // 128, 1) ** (-0.5)
    )
    inf, ins, inm, ine = adam_update(
        ffn_in_grad, ffn_in_first, ffn_in_second, ffn_in_master, ffn_in_ema, model_width ** (-0.5)
    )
    uf, us, um, ue = adam_update(
        ffn_out_grad,
        ffn_out_first,
        ffn_out_second,
        ffn_out_master,
        ffn_out_ema,
        hidden_units ** (-0.5),
    )
    sf, ss, sm, se = adam_update(
        small_grad, small_first, small_second, small_params, small_ema, SMALL_RATE
    )
    return (
        layer_out,
        input_grad,
        qkv_grad,
        out_grad,
        ffn_in_grad,
        ffn_out_grad,
        small_grad,
        grad_norm,
        qf,
        qs,
        qm,
        qm.astype(jnp.bfloat16),
        qe,
        of,
        osec,
        om,
        om.astype(jnp.bfloat16),
        oe,
        inf,
        ins,
        inm,
        inm.astype(jnp.bfloat16),
        ine,
        uf,
        us,
        um,
        um.astype(jnp.bfloat16),
        ue,
        sf,
        ss,
        sm,
        se,
    )


def solution(mesh):
    in_specs = (
        P("batch", "seq", None),
        P("batch", "seq", None),
        P("batch", None),
        P("batch", None),
        P("batch", None),
        P(),
        P(),
        P(),
        P(),
        P(),
        P(None, ("batch", "seq"), None),
        P(None, ("batch", "seq"), None),
        P(None, ("batch", "seq"), None),
        P(None, ("batch", "seq"), None),
        P(("batch", "seq"), None),
        P(("batch", "seq"), None),
        P(("batch", "seq"), None),
        P(("batch", "seq"), None),
        P(("batch", "seq"), None),
        P(("batch", "seq"), None),
        P(("batch", "seq"), None),
        P(("batch", "seq"), None),
        P(("batch", "seq"), None),
        P(("batch", "seq"), None),
        P(("batch", "seq"), None),
        P(("batch", "seq"), None),
        P(),
        P(),
        P(),
    )
    out_specs = (
        P("batch", "seq", None),
        P("batch", "seq", None),
        P(None, ("batch", "seq"), None),
        P(("batch", "seq"), None),
        P(("batch", "seq"), None),
        P(("batch", "seq"), None),
        P(),
        P(),
        P(None, ("batch", "seq"), None),
        P(None, ("batch", "seq"), None),
        P(None, ("batch", "seq"), None),
        P(None, ("batch", "seq"), None),
        P(None, ("batch", "seq"), None),
        P(("batch", "seq"), None),
        P(("batch", "seq"), None),
        P(("batch", "seq"), None),
        P(("batch", "seq"), None),
        P(("batch", "seq"), None),
        P(("batch", "seq"), None),
        P(("batch", "seq"), None),
        P(("batch", "seq"), None),
        P(("batch", "seq"), None),
        P(("batch", "seq"), None),
        P(("batch", "seq"), None),
        P(("batch", "seq"), None),
        P(("batch", "seq"), None),
        P(("batch", "seq"), None),
        P(("batch", "seq"), None),
        P(),
        P(),
        P(),
        P(),
    )
    return jax.shard_map(body, mesh=mesh, in_specs=in_specs, out_specs=out_specs, check_vma=False)
```

profile of v0, /device:TPU:0, one launch (start us, length us, event | category | flops | bytes accessed | tf_op | source)
XLA Modules:
  0.0 835.6 jit_solution(6887768412062514018)
XLA Ops:
  7.3 4.4 convolution_convert_fusion.1
  12.4 3.8 add_convert_fusion.4
  16.4 3.1 add_convert_fusion.3
  19.5 1.9 copy.102
  21.4 3.0 reshape.204
  25.3 34.2 %all-gather.5.cloned.1.call-done = bf16[4,512,768]{2,1,0:T(8,128)(2,1)} async-done(((bf16[4,256,768]{2,1,0:T(8,128)(2,1)}), bf16[4,512,768]{2,1,0:T(8,128)(2,1)}) %all-gather.5.cloned.1.call-update) | async-done | bytes 3145744 | tf_op jit(solution)/shard_map/all_gather | solution.py:142
  59.5 4.6 copy.103
  64.2 13.4 %fusion.12 = (f32[4,12,256]{2,1,0:T(8,128)S(1)}, f32[4,12,256,512]{3,2,1,0:T(8,128)}) fusion(pred[4,256,512]{2,1,0:T(8,128)(4,1)S(1)} %compare_or_fusion, bf16[4,512,12,64]{1,3,2,0:T(8,128)(2,1)} %bitcast.114, bf16[4,256,12,64]{1,0,3,2:T(4,128)(2,1)S(1)} %reshape.204), kind=kOutput, calls=%fused_computation.31 | convolution fusion | flops 824168448 | bytes 30457856 | tf_op jit(solution)/shard_map/bqhe,bkhe->bhqk/dot_general | solution.py:153
  77.6 11.8 %fusion = f32[4,12,256]{2,1,0:T(8,128)S(1)} fusion(f32[4,12,256]{2,1,0:T(8,128)S(1)} %get-tuple-element.149, f32[4,12,256,512]{3,2,1,0:T(8,128)} %get-tuple-element.150, pred[4,256,512]{2,1,0:T(8,128)(4,1)S(1)} %compare_or_fusion), kind=kLoop, calls=%fused_computation.6 | loop fusion | flops 25153536 | bytes 25788416 | tf_op jit(solution)/shard_map/reduce_sum | solution.py:163
  90.0 16.6 %all-gather.3.cloned.1.call-done = bf16[4,512,768]{2,1,0:T(8,128)(2,1)} async-done(((bf16[4,256,768]{2,1,0:T(8,128)(2,1)}), bf16[4,512,768]{2,1,0:T(8,128)(2,1)}) %all-gather.3.cloned.1.call-update) | async-done | bytes 3145744 | tf_op jit(solution)/shard_map/all_gather | solution.py:143
  106.6 4.7 copy.101
  111.3 12.0 %fusion.23 = bf16[4,256,12,64]{1,3,2,0:T(8,128)(2,1)S(1)} fusion(bf16[4,512,12,64]{1,3,2,0:T(8,128)(2,1)} %bitcast.116, f32[4,12,256]{2,1,0:T(8,128)S(1)} %fusion, f32[4,12,256]{2,1,0:T(8,128)S(1)} %get-tuple-element.149, f32[4,12,256,512]{3,2,1,0:T(8,128)} %get-tuple-element.150, pred[4,256,512]{2,1,0:T(8,128)(4,1)S(1)} %compare_or_fusion), kind=kOutput, calls=%fused_computation.75 | convolution fusion | flops 837550080 | bytes 30507008 | tf_op jit(solution)/shard_map/bhqk,bkhe->bqhe/dot_general | solution.py:166
  124.9 1.7 fusion.68
  128.3 35.4 %multiply_convert_fusion.1 = (bf16[1024,3072]{1,0:T(8,128)(2,1)S(1)}, f32[1024,3072]{1,0:T(8,128)}, f32[1024,3072]{1,0:T(8,128)}) fusion(f32[3072]{0:T(1024)S(1)} %slice.47, bf16[768,3072]{1,0:T(8,128)(2,1)S(1)} %bitcast.141, f32[1024,768]{1,0:T(8,128)S(1)} %get-tuple-element.152, f32[768]{0:T(1024)S(1)} %get-tuple-element.143, ...), kind=kOutput, calls=%fused_computation.14 | convolution fusion | flops 5043388416 | bytes 39348224 | tf_op jit(solution)/shard_map/dot_general | solution.py:47
  163.7 5.5 fusion.69
  170.6 1.8 fusion.17
  172.4 2.6 fusion.65
  177.6 17.9 %convert_reduce_fusion = (f32[3072]{0:T(1024)}, bf16[1024,3072]{1,0:T(8,128)(2,1)}) fusion(f32[1024,3072]{1,0:T(8,128)} %get-tuple-element.139, bf16[1024,768]{1,0:T(8,128)(2,1)S(1)} %get-tuple-element.131, bf16[3072,768]{1,0:T(8,128)(2,1)} %param.37, f32[1024,3072]{1,0:T(8,128)} %get-tuple-element.153, f32[3072]{0:T(1024)S(1)} %slice.47), kind=kOutput, calls=%fused_computation.11 | convolution fusion | flops 4885312512 | bytes 37773312 | tf_op jit(solution)/shard_map/dot_general | solution.py:57
  195.5 10.6 %multiply_reduce_fusion.4 = (f32[768]{0:T(1024)}, f32[1024]{0:T(1024)S(1)}, f32[768]{0:T(1024)}, f32[1024,768]{1,0:T(8,128)S(1)}) fusion(f32[1024,768]{1,0:T(8,128)S(1)} %get-tuple-element.152, f32[1024]{0:T(1024)S(1)} %fusion.49, f32[1024]{0:T(1024)S(1)} %broadcast_multiply_fusion.2, f32[768]{0:T(1024)S(1)} %get-tuple-element.144, ...), kind=kOutput, calls=%fused_computation.49 | convolution fusion | flops 4839699456 | bytes 20472832 | tf_op jit(solution)/shard_map/dot_general | solution.py:57
  211.3 2.6 convolution_convert_fusion
  213.9 1.8 copy.106
  215.7 2.4 reshape.209
  218.0 21.0 %multiply_reduce_fusion = (f32[4,12,256]{2,1,0:T(8,128)S(1)}, f32[4,12,256,512]{3,2,1,0:T(8,128)}) fusion(f32[4,12,256]{2,1,0:T(8,128)S(1)} %copy-done.31, f32[4,12,256,512]{3,2,1,0:T(8,128)} %get-tuple-element.150, pred[4,256,512]{2,1,0:T(8,128)(4,1)S(1)} %copy-done.11, bf16[4,512,12,64]{1,3,2,0:T(8,128)(2,1)} %bitcast.117, ...), kind=kOutput, calls=%fused_computation.1 | convolution fusion | flops 836751360 | bytes 55672832 | tf_op jit(solution)/shard_map/bqhe,bkhe->bhqk/dot_general | solution.py:206
  239.0 17.4 %multiply_convert_fusion = bf16[4,12,256,512]{3,2,1,0:T(8,128)(2,1)S(1)} fusion(f32[4,12,256,512]{3,2,1,0:T(8,128)} %get-tuple-element.158, f32[4,12,256]{2,1,0:T(8,128)S(1)} %get-tuple-element.157, f32[4,12,256]{2,1,0:T(8,128)S(1)} %copy-done.31, f32[4,12,256,512]{3,2,1,0:T(8,128)} %get-tuple-element.150, pred[4,256,512]{2,1,0:T(8,128)(4,1)S(1)} %copy-done.11), kind=kLoop, calls=%fused_computation | loop fusion | flops 37748736 | bytes 63537152 | tf_op jit(solution)/shard_map/convert_element_type | solution.py:210
  256.4 4.6 copy-done.1
  261.0 3.7 fusion.13
  266.2 14.0 %convert_bitcast_fusion = bf16[4,512,12,64]{1,3,2,0:T(8,128)(2,1)} fusion(f32[4,12,256]{2,1,0:T(8,128)S(1)} %copy-done.31, f32[4,12,256,512]{3,2,1,0:T(8,128)} %get-tuple-element.150, pred[4,256,512]{2,1,0:T(8,128)(4,1)S(1)} %copy-done.11, bf16[4,256,12,64]{1,0,3,2:T(4,128)(2,1)S(1)} %copy-done.17), kind=kOutput, calls=%fused_computation.51 | convolution fusion | flops 832045056 | bytes 30457856 | tf_op jit(solution)/shard_map/bhqk,bqhe->bkhe/dot_general | solution.py:203
  280.2 10.2 %convert_reduce_fusion.5 = (f32[12,64]{1,0:T(8,128)}, bf16[4,256,12,64]{1,3,2,0:T(8,128)(2,1)S(1)}) fusion(bf16[4,512,12,64]{1,3,2,0:T(8,128)(2,1)} %bitcast.115, bf16[4,12,256,512]{3,2,1,0:T(8,128)(2,1)} %copy-done.1), kind=kOutput, calls=%fused_computation.48 | convolution fusion | flops 808451328 | bytes 17304576 | tf_op jit(solution)/shard_map/bhqk,bkhe->bqhe/dot_general | solution.py:212
  292.5 2.8 fusion.70
  298.3 8.6 %fusion.55 = f32[768,3072]{1,0:T(8,128)} fusion(bf16[1024,3072]{1,0:T(8,128)(2,1)S(1)} %bitcast.121, f32[1024,768]{1,0:T(8,128)S(1)} %copy-done.3, f32[768]{0:T(1024)S(1)} %get-tuple-element.143, f32[768]{0:T(1024)S(1)} %get-tuple-element.144, f32[1024]{0:T(1024)S(1)} %fusion.49, f32[1024]{0:T(1024)S(1)} %broadcast_multiply_fusion.2), kind=kOutput, calls=%fused_computation.155 | convolution fusion | flops 4835770368 | bytes 18888704 | tf_op jit(solution)/shard_map/dot_general | solution.py:51
  307.0 7.7 fusion.71
  314.7 2.6 copy.110
  318.8 35.0 %reduce-scatter.5.cloned.1.call-done = bf16[4,256,12,64]{1,3,2,0:T(8,128)(2,1)} async-done(((bf16[4,512,12,64]{1,3,2,0:T(8,128)(2,1)}), bf16[4,256,12,64]{1,3,2,0:T(8,128)(2,1)}) %reduce-scatter.5.cloned.1.call-update) | async-done | bytes 1572880 | tf_op jit(solution)/shard_map/reduce_scatter | solution.py:223
  353.8 2.8 copy.112
  360.5 3.3 pad_maximum_fusion
  365.7 5.3 fusion.33
  371.4 42.1 %psum.39 = f32[9216]{0:T(1024)S(1)} all-reduce(f32[9216]{0:T(1024)S(1)} %constant_dynamic-update-slice_fusion), channel_id=1, replica_groups=mesh['batch'=16,'seq'=2] {'batch','seq'}, use_global_device_ids=true, to_apply=%region_30.31 | all-reduce | flops 9216 | bytes 73728 | tf_op jit(solution)/shard_map/psum | solution.py:259
  414.1 2.9 fusion.30
  418.5 4.8 add_convert_fusion.1
  423.3 374.0 %all-reduce.3.cloned.1.call-done = (f32[3,768,768]{2,1,0:T(8,128)}, f32[768,768]{1,0:T(8,128)}, f32[768,3072]{1,0:T(8,128)}, f32[3072,768]{1,0:T(8,128)}) async-done(((f32[3,768,768]{2,1,0:T(8,128)}, f32[768,768]{1,0:T(8,128)}, f32[768,3072]{1,0:T(8,128)}, f32[3072,768]{1,0:T(8,128)}), (f32[3,768,768]{2,1,0:T(8,128)}, f32[768,768]{1,0:T(8,128)}, f32[768,3072]{1,0:T(8,128)}, ...) | async-done | bytes 28311568 | tf_op jit(solution)/shard_map/psum | solution.py:259
  797.3 5.6 multiply_reduce_fusion.3
  802.9 3.7 multiply_reduce_fusion.8
  806.6 3.0 multiply_reduce_fusion.2
  809.7 3.0 multiply_reduce_fusion.1
  816.2 2.1 multiply_add_fusion.5
  819.0 1.7 multiply_add_fusion.7
  821.4 2.1 multiply_add_fusion.3
  824.2 2.1 multiply_add_fusion.1
  (228 shorter events, 34.3 us)
Async XLA Ops:
  7.2 117.7 %copy-start = (bf16[768,768]{1,0:T(8,128)(2,1)S(1)}, bf16[768,768]{1,0:T(8,128)(2,1)}, u32[]{:S(2)}) copy-start(bf16[768,768]{1,0:T(8,128)(2,1)} %param.35) | copy-start | bytes 3538948
  7.2 52.3 %all-gather.5.cloned.1.call-start = ((), (), s32[]{:S(2)}) async-start(), calls=%async_computation.3 | async-start | bytes 4718592 | tf_op jit(solution)/shard_map/all_gather | solution.py:142
  7.3 5.1 copy-start.66
  11.7 94.9 %all-gather.3.cloned.1.call-start = ((), (), s32[]{:S(2)}) async-start(), calls=%async_computation.2 | async-start | bytes 4718592 | tf_op jit(solution)/shard_map/all_gather | solution.py:143
  16.3 298.4 %reduce-scatter.3.cloned.1.call-start = ((), (), s32[]{:S(2)}) async-start(), calls=%async_computation.4 | async-start | bytes 4718592 | tf_op jit(solution)/shard_map/reduce_scatter | solution.py:220
  19.5 4.9 copy-start.55
  19.5 4.9 copy-start.56
  24.4 39.8 %copy-start.8 = (bf16[4,256,12,64]{1,0,3,2:T(4,128)(2,1)}, bf16[4,256,12,64]{1,0,3,2:T(4,128)(2,1)S(1)}, u32[]{:S(2)}) copy-start(bf16[4,256,12,64]{1,0,3,2:T(4,128)(2,1)S(1)} %reshape.204) | copy-start | bytes 4718596
  25.3 86.0 %copy-start.10 = (pred[4,256,512]{2,1,0:T(8,128)(4,1)}, pred[4,256,512]{2,1,0:T(8,128)(4,1)S(1)}, u32[]{:S(2)}) copy-start(pred[4,256,512]{2,1,0:T(8,128)(4,1)S(1)} %compare_or_fusion) | copy-start | bytes 1572868
  124.9 38.8 %slice-start.5 = ((s8[4718592]{0:T(1024)(128)(4,1)}), s8[4194304]{0:T(1024)(128)(4,1)S(1)}, s32[]{:S(2)}) async-start(s8[4718592]{0:T(1024)(128)(4,1)} %bitcast.138), calls=%async_computation.12 | async-start | bytes 8388608
  126.6 79.4 %copy-start.2 = (f32[1024,768]{1,0:T(8,128)}, f32[1024,768]{1,0:T(8,128)S(1)}, u32[]{:S(2)}) copy-start(f32[1024,768]{1,0:T(8,128)S(1)} %get-tuple-element.152) | copy-start | bytes 9437188
  128.3 35.4 %copy-start.63 = (f32[768]{0:T(1024)S(1)}, f32[768]{0:T(1024)}, u32[]{:S(2)}) copy-start(f32[768]{0:T(1024)} %get-tuple-element.142) | copy-start | bytes 9220
  128.3 35.4 %slice-start.6 = ((s8[4718592]{0:T(1024)(128)(4,1)}), s8[524288]{0:T(1024)(128)(4,1)S(1)}, s32[]{:S(2)}) async-start(s8[4718592]{0:T(1024)(128)(4,1)} %bitcast.138), calls=%async_computation.13 | async-start | bytes 1048576
  163.7 5.5 copy-start.70
  177.6 17.9 %copy-start.24 = (bf16[1024,768]{1,0:T(8,128)(2,1)}, bf16[1024,768]{1,0:T(8,128)(2,1)S(1)}, u32[]{:S(2)}) copy-start(bf16[1024,768]{1,0:T(8,128)(2,1)S(1)} %get-tuple-element.131) | copy-start | bytes 4718596
  239.0 22.0 %copy-start.9 = (bf16[4,256,12,64]{1,0,3,2:T(4,128)(2,1)S(1)}, bf16[4,256,12,64]{1,0,3,2:T(4,128)(2,1)}, u32[]{:S(2)}) copy-start(bf16[4,256,12,64]{1,0,3,2:T(4,128)(2,1)} %copy-done.8) | copy-start | bytes 4718596
  264.8 89.1 %reduce-scatter.5.cloned.1.call-start = ((), (), s32[]{:S(2)}) async-start(), calls=%async_computation.5 | async-start | bytes 4718592 | tf_op jit(solution)/shard_map/reduce_scatter | solution.py:223
  280.2 517.1 %all-reduce.3.cloned.1.call-start = ((), (), s32[]{:S(2)}) async-start(), calls=%async_computation.6 | async-start | bytes 56623104 | tf_op jit(solution)/shard_map/psum | solution.py:259
  295.3 11.6 %slice-start.9 = ((s8[6291456]{0:T(1024)(128)(4,1)}), s8[4194304]{0:T(1024)(128)(4,1)S(1)}, s32[]{:S(2)}) async-start(s8[6291456]{0:T(1024)(128)(4,1)} %bitcast.149), calls=%async_computation.16 | async-start | bytes 8388608
  298.3 8.6 %copy-start.25 = (bf16[1024,768]{1,0:T(8,128)(2,1)S(1)}, bf16[1024,768]{1,0:T(8,128)(2,1)}, u32[]{:S(2)}) copy-start(bf16[1024,768]{1,0:T(8,128)(2,1)} %copy-done.24) | copy-start | bytes 4718596
  298.3 8.6 %slice-start.10 = ((s8[6291456]{0:T(1024)(128)(4,1)}), s8[2097152]{0:T(1024)(128)(4,1)S(1)}, s32[]{:S(2)}) async-start(s8[6291456]{0:T(1024)(128)(4,1)} %bitcast.149), calls=%async_computation.17 | async-start | bytes 4194304
  365.7 5.3 copy-start.14
  365.7 5.7 copy-start.60
  365.7 5.7 copy-start.59
  365.7 5.7 copy-start.62
  365.7 48.4 %copy-start.22 = (bf16[96,8,4,256]{3,1,2,0:T(8,128)(2,1)S(1)}, bf16[96,8,4,256]{3,1,2,0:T(8,128)(2,1)}, u32[]{:S(2)}) copy-start(bf16[96,8,4,256]{3,1,2,0:T(8,128)(2,1)} %copy.121) | copy-start | bytes 4718596
  797.3 9.3 %copy-start.13 = (f32[768,3072]{1,0:T(8,128)S(1)}, f32[768,3072]{1,0:T(8,128)}, u32[]{:S(2)}) copy-start(f32[768,3072]{1,0:T(8,128)} %get-tuple-element.103) | copy-start | bytes 28311556
  797.3 12.3 %slice-start = ((s8[9437184]{0:T(1024)(128)(4,1)}), s8[4194304]{0:T(1024)(128)(4,1)S(1)}, s32[]{:S(2)}) async-start(s8[9437184]{0:T(1024)(128)(4,1)} %bitcast.118), calls=%async_computation.7 | async-start | bytes 8388608
  797.3 12.3 %slice-start.1 = ((s8[9437184]{0:T(1024)(128)(4,1)}), s8[4194304]{0:T(1024)(128)(4,1)S(1)}, s32[]{:S(2)}) async-start(s8[9437184]{0:T(1024)(128)(4,1)} %bitcast.118), calls=%async_computation.8 | async-start | bytes 8388608
  809.6 6.5 copy-start.41
  809.6 6.5 copy-start.42
  809.6 6.5 copy-start.43
  809.7 9.4 %copy-start.46 = (f32[24,768]{1,0:T(8,128)S(1)}, f32[24,768]{1,0:T(8,128)}, u32[]{:S(2)}) copy-start(f32[24,768]{1,0:T(8,128)} %param.46) | copy-start | bytes 221188
  809.7 9.4 %copy-start.47 = (f32[24,768]{1,0:T(8,128)S(1)}, f32[24,768]{1,0:T(8,128)}, u32[]{:S(2)}) copy-start(f32[24,768]{1,0:T(8,128)} %param.43) | copy-start | bytes 221188
  812.7 8.7 %copy-start.33 = (f32[24,3072]{1,0:T(8,128)S(1)}, f32[24,3072]{1,0:T(8,128)}, u32[]{:S(2)}) copy-start(f32[24,3072]{1,0:T(8,128)} %param.50) | copy-start | bytes 884740
  812.7 8.7 %copy-start.34 = (f32[24,3072]{1,0:T(8,128)S(1)}, f32[24,3072]{1,0:T(8,128)}, u32[]{:S(2)}) copy-start(f32[24,3072]{1,0:T(8,128)} %param.47) | copy-start | bytes 884740
  812.7 8.7 %copy-start.35 = (f32[24,3072]{1,0:T(8,128)S(1)}, f32[24,3072]{1,0:T(8,128)}, u32[]{:S(2)}) copy-start(f32[24,3072]{1,0:T(8,128)} %param.49) | copy-start | bytes 884740
  812.7 8.7 %copy-start.36 = (f32[24,3072]{1,0:T(8,128)S(1)}, f32[24,3072]{1,0:T(8,128)}, u32[]{:S(2)}) copy-start(f32[24,3072]{1,0:T(8,128)} %param.48) | copy-start | bytes 884740
  816.2 8.0 copy-start.37
  816.2 8.0 copy-start.38
  816.2 8.0 copy-start.39
  816.2 8.0 copy-start.40
  818.3 8.0 copy-start.30
  820.7 5.6 copy-start.32
  821.4 5.6 copy-start.45
  821.4 5.6 copy-start.50
  821.4 5.6 copy-start.51
  821.4 5.6 copy-start.52
  (39 other events, 102.6 us)
Sparse Core Ops, SparseCore 0:
  11.9 47.6 all-gather.4
  61.6 44.9 all-gather.2
  264.9 43.3 reduce-scatter.2
  310.5 43.3 reduce-scatter.4
  364.0 433.2 all-reduce.2
where the time goes:
time: 840 us; the launch traced here: 836 us
  waiting for transfers between devices  460 us (55%)
  matrix products  196 us (23%)
  other arithmetic  70.6 us (8%)
  local copies, waits for them, and re-layouts  47.2 us (6%)
  blocking collectives  42.1 us (5%)
  between operations  19.5 us (2%)
    psum x1, waiting for transfers between devices, body(): lax.psum((g_qkv, g_attn, g_inner, g_outer, small_terms), ('batch', 'seq'))  374 us
    dot_general x6, matrix products, product(): return jnp.dot(left, right, preferred_element_type=jnp.float32)  53.9 us
    dot_general x6, matrix products, product_right_t(): lax.dot_general(left, right, (((1,), (1,)), ((), ())), preferred_element_...  44 us
    psum x1, blocking collectives, body(): lax.psum((g_qkv, g_attn, g_inner, g_outer, small_terms), ('batch', 'seq'))  42.1 us
    reduce_scatter x1, waiting for transfers between devices, body(): lax.psum_scatter(d_value.astype(jnp.bfloat16), 'seq', scatter_dimension=1...  35 us
    all_gather x1, waiting for transfers between devices, body(): lax.all_gather(key_low, 'seq', axis=1, tiled=True)  34.2 us
    dot_general x6, matrix products, product_left_t(): lax.dot_general(left, right, (((0,), (0,)), ((), ())), preferred_element_...  23.7 us
    dot_general x1, matrix products, body(): jnp.einsum('bqhe,bkhe->bhqk', d_context, value_heads, preferred_element_t...  21 us
  transfers between devices with their start and end apart: 5, of which 4 were waited for; matrix products, arithmetic and copies ran while one was open for 13% of the time, Pallas kernels for 0%

commit v1 on v0

--- a/solution.py
+++ b/solution.py
@@ -69,6 +69,41 @@
     )
     ema_new = EMA_KEEP * ema_old + (1.0 - EMA_KEEP) * master_new
     return (first_new, second_new, master_new, ema_new)
+
+
+AXES = ("batch", "seq")
+
+
+def partner_swap(values, bit):
+    count = lax.axis_size(AXES)
+    return lax.ppermute(values, AXES, [(place, place ^ (1 << bit)) for place in range(count)])
+
+
+def bit_order():
+    bits = lax.axis_size(AXES).bit_length() - 1
+    return list(range(1, bits)) + [0]
+
+
+def scatter_sum(rows):
+    order = bit_order()
+    place = lax.axis_index(AXES)
+    left = list(reversed(range(len(order))))
+    held = rows.astype(jnp.bfloat16).reshape((2,) * len(order) + rows.shape[1:])
+    for bit in order:
+        axis = left.index(bit)
+        mine = (place >> bit) & 1
+        keep = lax.dynamic_index_in_dim(held, mine, axis, keepdims=False)
+        send = lax.dynamic_index_in_dim(held, 1 - mine, axis, keepdims=False)
+        total = keep.astype(jnp.float32) + partner_swap(send, bit).astype(jnp.float32)
+        left.remove(bit)
+        held = total.astype(jnp.bfloat16) if left else total
+    return held
+
+
+def butterfly_sum(values):
+    for bit in bit_order():
+        values = values + partner_swap(values, bit)
+    return values
 
 
 def body(
@@ -107,13 +142,14 @@
     heads = model_width // HD
     head_scale = HD ** (-0.5)
     seq_place = lax.axis_index("seq")
-    local_x, local_cot = (tables_in, out_cot)
+    swap = lambda rows: lax.all_to_all(rows, "seq", split_axis=0, concat_axis=1, tiled=True)
+    unswap = lambda rows: lax.all_to_all(rows, "seq", split_axis=1, concat_axis=0, tiled=True)
+    local_x, local_cot = (swap(tables_in), swap(out_cot))
     tab_count = local_x.shape[0]
     block_rows = local_x.shape[1]
-    seg_keys, row_keys, col_keys = (segment_ids, row_ids, col_ids)
-    seg_query = lax.dynamic_slice_in_dim(segment_ids, seq_place * block_rows, block_rows, 1)
-    row_query = lax.dynamic_slice_in_dim(row_ids, seq_place * block_rows, block_rows, 1)
-    col_query = lax.dynamic_slice_in_dim(col_ids, seq_place * block_rows, block_rows, 1)
+    own = lambda ids: lax.dynamic_slice_in_dim(ids, seq_place * tab_count, tab_count, 0)
+    seg_keys, row_keys, col_keys = (own(segment_ids), own(row_ids), own(col_ids))
+    seg_query, row_query, col_query = (seg_keys, row_keys, col_keys)
     row_count = tab_count * block_rows
     (
         gain_one,
@@ -138,10 +174,7 @@
         .astype(jnp.bfloat16)
         .reshape(tab_count, block_rows, model_width)
     )
-    key_all, value_all = (
-        lax.all_gather(key_low, "seq", axis=1, tiled=True),
-        lax.all_gather(value_low, "seq", axis=1, tiled=True),
-    )
+    key_all, value_all = key_low, value_low
     rows_key = key_all.shape[1]
     query_heads = query_low.reshape(tab_count, block_rows, heads, HD)
     key_heads = key_all.reshape(tab_count, rows_key, heads, HD)
@@ -177,7 +210,7 @@
     branch = product(active_low, ffn_out_weight) + bias_ffn
     second_sum = normed + branch
     result, second_back = jax.vjp(norm_rows, second_sum, gain_two, shift_two)
-    layer_out = result.astype(jnp.bfloat16).reshape(tab_count, block_rows, model_width)
+    layer_out = unswap(result.astype(jnp.bfloat16).reshape(tab_count, block_rows, model_width))
     back_rows = local_cot.reshape(row_count, model_width).astype(jnp.float32)
     d_second, d_gain_two, d_shift_two = second_back(back_rows)
     d_branch = d_second.astype(jnp.bfloat16)
@@ -216,14 +249,6 @@
         jnp.einsum("bhqk,bqhe->bkhe", d_scores_low, query_heads, preferred_element_type=jnp.float32)
         * head_scale
     )
-    d_key, d_value = (
-        lax.psum_scatter(d_key.astype(jnp.bfloat16), "seq", scatter_dimension=1, tiled=True).astype(
-            jnp.float32
-        ),
-        lax.psum_scatter(
-            d_value.astype(jnp.bfloat16), "seq", scatter_dimension=1, tiled=True
-        ).astype(jnp.float32),
-    )
     d_query_low = d_query.astype(jnp.bfloat16).reshape(row_count, model_width)
     d_key_low = d_key.astype(jnp.bfloat16).reshape(row_count, model_width)
     d_value_low = d_value.astype(jnp.bfloat16).reshape(row_count, model_width)
@@ -242,7 +267,7 @@
         + product_right_t(d_key_low, qkv_weight[1])
         + product_right_t(d_value_low, qkv_weight[2])
     )
-    input_grad = d_input.astype(jnp.bfloat16).reshape(tab_count, block_rows, model_width)
+    input_grad = unswap(d_input.astype(jnp.bfloat16).reshape(tab_count, block_rows, model_width))
     small_terms = jnp.concatenate(
         [
             d_gain_one,
@@ -256,29 +281,21 @@
             d_bias_inner,
         ]
     )
-    full_qkv, full_attn, full_inner, full_outer, small_sum = lax.psum(
-        (g_qkv, g_attn, g_inner, g_outer, small_terms), ("batch", "seq")
-    )
-    total_sq = (
-        jnp.sum(full_qkv * full_qkv)
-        + jnp.sum(full_attn * full_attn)
-        + jnp.sum(full_inner * full_inner)
-        + jnp.sum(full_outer * full_outer)
-        + jnp.sum(small_sum * small_sum)
-    )
-    shard_index = lax.axis_index(("batch", "seq"))
-    share_qkv = lax.dynamic_slice_in_dim(
-        full_qkv, shard_index * qkv_master.shape[1], qkv_master.shape[1], 1
-    )
-    share_attn = lax.dynamic_slice_in_dim(
-        full_attn, shard_index * out_master.shape[0], out_master.shape[0], 0
-    )
-    share_inner = lax.dynamic_slice_in_dim(
-        full_inner, shard_index * ffn_in_master.shape[0], ffn_in_master.shape[0], 0
-    )
-    share_outer = lax.dynamic_slice_in_dim(
-        full_outer, shard_index * ffn_out_master.shape[0], ffn_out_master.shape[0], 0
-    )
+    shards = lax.axis_size(AXES)
+    share_outer = scatter_sum(g_outer.reshape(shards, -1)).reshape(ffn_out_master.shape)
+    share_inner = scatter_sum(g_inner.reshape(shards, -1)).reshape(ffn_in_master.shape)
+    share_attn = scatter_sum(g_attn.reshape(shards, -1)).reshape(out_master.shape)
+    share_qkv = scatter_sum(
+        g_qkv.reshape(3, shards, -1).swapaxes(0, 1).reshape(shards, -1)
+    ).reshape(qkv_master.shape)
+    small_sum = butterfly_sum(small_terms)
+    share_sq = (
+        jnp.sum(share_qkv * share_qkv)
+        + jnp.sum(share_attn * share_attn)
+        + jnp.sum(share_inner * share_inner)
+        + jnp.sum(share_outer * share_outer)
+    )
+    total_sq = butterfly_sum(share_sq.reshape(1))[0] + jnp.sum(small_sum * small_sum)
     grad_norm = jnp.sqrt(total_sq)
     clip_limit = math.sqrt(
         float(

time: 840 us -> 611 us (0.73)
  waiting for transfers between devices: 460 us -> 134 us
  local copies, waits for them, and re-layouts: 47.2 us -> 131 us
  starting transfers between devices: 0.21 us -> 53.2 us
  blocking collectives: 42.1 us -> 0 us
  other arithmetic: 70.6 us -> 85.8 us
  matrix products: 196 us -> 186 us
  between operations: 19.5 us -> 9.71 us
    psum x1 -> x0, waiting for transfers between devices: 374 us -> none  [body(): lax.psum((g_qkv, g_attn, g_inner, g_outer, small_terms), ('batch', 'seq'))]
    ppermute x0 -> x30, waiting for transfers between devices: none -> 100 us  [partner_swap(): lax.ppermute(values, AXES, [(place, place ^ 1 << bit) for place in range(...]
    convert_element_type x0 -> x10, local copies, waits for them, and re-layouts: none -> 57.5 us  [the longest x5 44 us: scatter_sum(): held = rows.astype(jnp.bfloat16).reshape((2,) * len(order) + rows.shape[1:])]
    all_gather x2 -> x0, waiting for transfers between devices: 50.9 us -> none  [the longest x1 34.2 us: body(): lax.all_gather(key_low, 'seq', axis=1, tiled=True)]
    psum x1 -> x0, blocking collectives: 42.1 us -> none  [body(): lax.psum((g_qkv, g_attn, g_inner, g_outer, small_terms), ('batch', 'seq'))]
    ppermute x0 -> x30, starting transfers between devices: none -> 35.5 us  [partner_swap(): lax.ppermute(values, AXES, [(place, place ^ 1 << bit) for place in range(...]
    reduce_scatter x2 -> x0, waiting for transfers between devices: 35 us -> none  [the longest x1 35 us: body(): lax.psum_scatter(d_value.astype(jnp.bfloat16), 'seq', scatter_dimension=1...]
    all_to_all x0 -> x4, waiting for transfers between devices: none -> 33.8 us  [the longest x2 18.7 us: body(): lax.all_to_all(rows, 'seq', split_axis=0, concat_axis=1, tiled=True)]
  transfers between devices with their start and end apart: 5 -> 34, of which waited for: 4 -> 17; matrix products, arithmetic and copies ran while one was open for 13% -> 27% of each run, Pallas kernels for 0% -> 0%
where the time goes in v1:
time: 611 us; the launch traced here: 599 us
  matrix products  186 us (30%)
  waiting for transfers between devices  134 us (22%)
  local copies, waits for them, and re-layouts  131 us (21%)
  other arithmetic  85.8 us (14%)
  starting transfers between devices  53.2 us (9%)
  between operations  9.71 us (2%)
    ppermute x30, waiting for transfers between devices, partner_swap(): lax.ppermute(values, AXES, [(place, place ^ 1 << bit) for place in range(...  100 us
    dot_general x6, matrix products, product(): return jnp.dot(left, right, preferred_element_type=jnp.float32)  53.8 us
    convert_element_type x5, local copies, waits for them, and re-layouts, scatter_sum(): held = rows.astype(jnp.bfloat16).reshape((2,) * len(order) + rows.shape[1:])  44 us
    dot_general x6, matrix products, product_right_t(): lax.dot_general(left, right, (((1,), (1,)), ((), ())), preferred_element_...  37.6 us
    ppermute x30, starting transfers between devices, partner_swap(): lax.ppermute(values, AXES, [(place, place ^ 1 << bit) for place in range(...  35.5 us
    dot_general x6, matrix products, product_left_t(): lax.dot_general(left, right, (((0,), (0,)), ((), ())), preferred_element_...  24.6 us
    convert_element_type x1, other arithmetic, body(): d_scores_low = d_scores.astype(jnp.bfloat16)  21.9 us
    squeeze x16, local copies, waits for them, and re-layouts, scatter_sum(): send = lax.dynamic_index_in_dim(held, 1 - mine, axis, keepdims=False)  21.1 us
  transfers between devices with their start and end apart: 34, of which 17 were waited for; matrix products, arithmetic and copies ran while one was open for 27% of the time, Pallas kernels for 0%

profile of v1, /device:TPU:0, one launch (start us, length us, event | category | flops | bytes accessed | tf_op | source)
XLA Modules:
  0.0 599.5 jit_solution(8858670997619091150)
XLA Ops:
  0.7 4.3 all-to-all-start
  6.6 18.7 %all-to-all-done = bf16[4,256,768]{2,1,0:T(8,128)(2,1)S(1)} async-done(((bf16[4,256,768]{2,1,0:T(8,128)(2,1)}), bf16[4,256,768]{2,1,0:T(8,128)(2,1)S(1)}, u32[]{:S(2)}, u32[]{:S(2)}) %all-to-all-start) | async-done | bytes 1572896 | tf_op jit(solution)/shard_map/all_to_all | solution.py:145
  25.2 4.6 all-to-all-start.2
  31.1 3.8 add_convert_fusion.3
  39.0 4.3 add_convert_fusion.4
  47.4 3.1 convolution_convert_fusion.3
  55.0 4.0 copy.116
  59.0 10.5 %fusion.12 = (f32[2,12,512]{2,1,0:T(8,128)S(1)}, f32[2,12,512,512]{2,3,1,0:T(8,128)}) fusion(pred[2,512,512]{1,2,0:T(8,128)(4,1)S(1)} %compare_or_fusion, bf16[2,512,12,64]{1,0,3,2:T(2,128)(2,1)S(1)} %reshape_reshape.7, bf16[2,512,12,64]{1,0,3,2:T(2,128)(2,1)S(1)} %copy-done.6), kind=kOutput, calls=%fused_computation.29 | convolution fusion | flops 824168448 | bytes 28884992 | tf_op jit(solution)/shard_map/bqhe,bkhe->bhqk/dot_general | solution.py:186
  69.5 11.1 %fusion = f32[2,12,512]{2,1,0:T(8,128)S(1)} fusion(f32[2,12,512]{2,1,0:T(8,128)S(1)} %get-tuple-element.87, f32[2,12,512,512]{2,3,1,0:T(8,128)} %get-tuple-element.88, pred[2,512,512]{1,2,0:T(8,128)(4,1)S(1)} %compare_or_fusion), kind=kLoop, calls=%fused_computation.6 | loop fusion | flops 25153536 | bytes 25788416 | tf_op jit(solution)/shard_map/reduce_sum | solution.py:196
  81.3 12.0 %fusion.30 = bf16[2,512,12,64]{1,3,2,0:T(8,128)(2,1)S(1)} fusion(f32[2,12,512]{2,1,0:T(8,128)S(1)} %fusion, f32[2,12,512]{2,1,0:T(8,128)S(1)} %get-tuple-element.87, f32[2,12,512,512]{2,3,1,0:T(8,128)} %get-tuple-element.88, pred[2,512,512]{1,2,0:T(8,128)(4,1)S(1)} %compare_or_fusion, bf16[2,512,12,64]{1,0,3,2:T(2,128)(2,1)S(1)} %copy-done.11), kind=kOutput, calls=%fused_computation.87 | convolution fusion | flops 837550080 | bytes 28934144 | tf_op jit(solution)/shard_map/bhqk,bkhe->bqhe/dot_general | solution.py:199
  98.2 35.4 %multiply_convert_fusion.1 = (bf16[1024,3072]{1,0:T(8,128)(2,1)S(1)}, f32[1024,3072]{1,0:T(8,128)}, f32[1024,3072]{1,0:T(8,128)}) fusion(f32[3072]{0:T(1024)S(1)} %slice.47, bf16[768,3072]{1,0:T(8,128)(2,1)S(1)} %bitcast.243, f32[1024,768]{1,0:T(8,128)S(1)} %get-tuple-element.90, f32[768]{0:T(1024)S(1)} %get-tuple-element.81, ...), kind=kOutput, calls=%fused_computation.14 | convolution fusion | flops 5043388416 | bytes 39348224 | tf_op jit(solution)/shard_map/dot_general | solution.py:47
  133.6 5.5 fusion.97
  148.0 6.9 %convolution_convert_fusion = bf16[3072,768]{1,0:T(8,128)(2,1)} fusion(bf16[1024,3072]{1,0:T(8,128)(2,1)S(1)} %get-tuple-element.68, bf16[1024,768]{1,0:T(8,128)(2,1)S(1)} %get-tuple-element.61), kind=kOutput, calls=%fused_computation.30 | convolution fusion | flops 4834197504 | bytes 12582912 | tf_op jit(solution)/shard_map/dot_general | solution.py:51
  154.9 16.9 %convert_reduce_fusion = (f32[3072]{0:T(1024)S(1)}, bf16[1024,3072]{1,0:T(8,128)(2,1)}) fusion(f32[1024,3072]{1,0:T(8,128)} %get-tuple-element.69, bf16[1024,768]{1,0:T(8,128)(2,1)S(1)} %get-tuple-element.61, bf16[3072,768]{1,0:T(8,128)(2,1)} %param.37, f32[1024,3072]{1,0:T(8,128)} %get-tuple-element.91, f32[3072]{0:T(1024)S(1)} %slice.47), kind=kOutput, calls=%fused_computation.11 | convolution fusion | flops 4885312512 | bytes 37773312 | tf_op jit(solution)/shard_map/dot_general | solution.py:57
  171.8 10.1 %multiply_reduce_fusion.1 = (f32[768]{0:T(1024)S(1)}, f32[1024]{0:T(1024)S(1)}, f32[768]{0:T(1024)S(1)}, f32[1024,768]{1,0:T(8,128)S(1)}) fusion(f32[1024,768]{1,0:T(8,128)S(1)} %get-tuple-element.90, f32[1024]{0:T(1024)S(1)} %fusion.78, f32[1024]{0:T(1024)S(1)} %broadcast_multiply_fusion.2, f32[768]{0:T(1024)S(1)} %get-tuple-element.82, ...), kind=kOutput, calls=%fused_computation.48 | convolution fusion | flops 4839699456 | bytes 20472832 | tf_op jit(solution)/shard_map/dot_general | solution.py:57
  182.0 8.0 %convolution_convert_fusion.1 = bf16[768,3072]{1,0:T(8,128)(2,1)} fusion(bf16[1024,3072]{1,0:T(8,128)(2,1)S(1)} %copy-done.58, f32[1024,768]{1,0:T(8,128)S(1)} %get-tuple-element.90, f32[768]{0:T(1024)S(1)} %get-tuple-element.81, f32[768]{0:T(1024)S(1)} %get-tuple-element.82, f32[1024]{0:T(1024)S(1)} %fusion.78, f32[1024]{0:T(1024)S(1)} %broadcast_multiply_fusion.2), kind=kOutput, calls=%fused_computation.31 | convolution fusion | flops 4838129664 | bytes 14170112 | tf_op jit(solution)/shard_map/dot_general | solution.py:51
  203.2 12.9 %convert_reduce_fusion.3 = (f32[12,64]{1,0:T(8,128)S(1)}, bf16[2,512,12,64]{1,3,2,0:T(8,128)(2,1)}) fusion(f32[2,12,512]{2,1,0:T(8,128)S(1)} %copy-done.32, f32[2,12,512,512]{2,3,1,0:T(8,128)} %get-tuple-element.88, pred[2,512,512]{1,2,0:T(8,128)(4,1)S(1)} %copy-done.9, bf16[2,512,12,64]{1,0,3,2:T(2,128)(2,1)} %reshape.279), kind=kOutput, calls=%fused_computation.46 | convolution fusion | flops 832830720 | bytes 28888064 | tf_op jit(solution)/shard_map/bhqk,bqhe->bkhe/dot_general | solution.py:236
  216.2 18.1 %multiply_reduce_fusion = (f32[2,12,512]{2,1,0:T(8,128)S(1)}, f32[2,12,512,512]{2,3,1,0:T(8,128)}) fusion(f32[2,12,512]{2,1,0:T(8,128)S(1)} %copy-done.32, f32[2,12,512,512]{2,3,1,0:T(8,128)} %get-tuple-element.88, pred[2,512,512]{1,2,0:T(8,128)(4,1)S(1)} %copy-done.9, bf16[2,512,12,64]{1,0,3,2:T(2,128)(2,1)S(1)} %copy-done.12, ...), kind=kOutput, calls=%fused_computation.1 | convolution fusion | flops 836751360 | bytes 54099968 | tf_op jit(solution)/shard_map/bqhe,bkhe->bhqk/dot_general | solution.py:239
  234.3 21.9 %multiply_convert_fusion = bf16[2,12,512,512]{2,3,1,0:T(8,128)(2,1)} fusion(f32[2,12,512,512]{2,3,1,0:T(8,128)} %get-tuple-element.96, f32[2,12,512]{2,1,0:T(8,128)S(1)} %get-tuple-element.95, f32[2,12,512]{2,1,0:T(8,128)S(1)} %copy-done.32, f32[2,12,512,512]{2,3,1,0:T(8,128)} %get-tuple-element.88, pred[2,512,512]{1,2,0:T(8,128)(4,1)S(1)} %copy-done.9), kind=kLoop, calls=%fused_computation | loop fusion | flops 37748736 | bytes 63537152 | tf_op jit(solution)/shard_map/convert_element_type | solution.py:243
  256.1 9.8 %fusion.29 = bf16[2,512,12,64]{1,3,2,0:T(8,128)(2,1)} fusion(bf16[2,12,512,512]{2,3,1,0:T(8,128)(2,1)} %multiply_convert_fusion, bf16[2,512,12,64]{1,0,3,2:T(2,128)(2,1)S(1)} %copy-done.7), kind=kOutput, calls=%fused_computation.86 | convolution fusion | flops 806879232 | bytes 15728640 | tf_op jit(solution)/shard_map/bhqk,bqhe->bkhe/dot_general | solution.py:249
  265.9 6.8 %convert_reduce_fusion.4 = (f32[12,64]{1,0:T(8,128)S(1)}, bf16[2,512,12,64]{1,3,2,0:T(8,128)(2,1)S(1)}) fusion(bf16[2,12,512,512]{2,3,1,0:T(8,128)(2,1)} %multiply_convert_fusion, bf16[2,512,12,64]{1,0,3,2:T(2,128)(2,1)S(1)} %copy-done.5), kind=kOutput, calls=%fused_computation.47 | convolution fusion | flops 808451328 | bytes 15731712 | tf_op jit(solution)/shard_map/bhqk,bkhe->bqhe/dot_general | solution.py:245
  277.2 4.5 fusion.50
  284.4 3.7 all-to-all-start.1
  288.1 10.7 %convert_element_type.463 = bf16[2,2,2,2,2,73728]{5,4,3,2,1,0:T(2,128)(2,1)} reshape(bf16[3072,768]{1,0:T(8,128)(2,1)} %convolution_convert_fusion) | data formatting | bytes 9437184 | tf_op jit(solution)/shard_map/convert_element_type | solution.py:91
  298.8 11.7 %convert_element_type.442 = bf16[2,2,2,2,2,73728]{5,4,3,2,1,0:T(2,128)(2,1)} reshape(bf16[768,3072]{1,0:T(8,128)(2,1)} %convolution_convert_fusion.1) | data formatting | bytes 9437184 | tf_op jit(solution)/shard_map/convert_element_type | solution.py:91
  310.6 3.8 convert_element_type.421
  316.7 3.1 copy.128
  328.9 4.7 dynamic-slice_bitcast_fusion.1
  333.6 4.8 dynamic-slice_bitcast_fusion
  338.9 3.0 copy.125
  359.6 5.3 copy.134
  364.9 12.5 %convert_element_type.400 = bf16[2,2,2,2,2,55296]{5,4,3,2,1,0:T(2,128)(2,1)} reshape(bf16[32,3,18432]{2,1,0:T(4,128)(2,1)} %copy.134) | data formatting | bytes 7077888 | tf_op jit(solution)/shard_map/convert_element_type | solution.py:91
  381.6 4.2 dynamic-slice_bitcast_fusion.2
  406.0 5.1 all-to-all-start.3
  416.4 15.2 %all-to-all-done.3 = bf16[2,512,768]{2,0,1:T(2,128)(2,1)} async-done(((bf16[2,512,768]{2,0,1:T(2,128)(2,1)}), bf16[2,512,768]{2,0,1:T(2,128)(2,1)}, u32[]{:S(2)}, u32[]{:S(2)}) %all-to-all-start.3) | async-done | bytes 1572896 | tf_op jit(solution)/shard_map/all_to_all | solution.py:146
  431.5 2.9 copy.130
  435.1 3.8 fusion.15
  440.2 4.2 fusion.13
  446.7 15.5 %collective-permute-done.1 = bf16[2,2,2,55296]{3,2,1,0:T(2,128)(2,1)S(1)} collective-permute-done((bf16[2,2,2,55296]{3,2,1,0:T(2,128)(2,1)S(1)}, bf16[2,2,2,55296]{3,2,1,0:T(2,128)(2,1)S(1)}, u32[]{:S(2)}, u32[]{:S(2)}) %collective-permute-start.1) | collective-permute-done | bytes 884768 | tf_op jit(solution)/shard_map/ppermute | solution.py:79
  465.5 4.1 fusion.14
  469.6 4.1 collective-permute-done.2
  476.3 7.2 %collective-permute-done.3 = bf16[2,55296]{1,0:T(2,128)(2,1)S(1)} collective-permute-done((bf16[2,55296]{1,0:T(2,128)(2,1)S(1)}, bf16[2,55296]{1,0:T(2,128)(2,1)S(1)}, u32[]{:S(2)}, u32[]{:S(2)}) %collective-permute-start.3) | collective-permute-done | bytes 221216 | tf_op jit(solution)/shard_map/ppermute | solution.py:79
  485.0 25.7 %collective-permute-done.11 = bf16[2,2,2,73728]{3,2,1,0:T(2,128)(2,1)S(1)} collective-permute-done((bf16[2,2,2,73728]{3,2,1,0:T(2,128)(2,1)S(1)}, bf16[2,2,2,73728]{3,2,1,0:T(2,128)(2,1)S(1)}, u32[]{:S(2)}, u32[]{:S(2)}) %collective-permute-start.11) | collective-permute-done | bytes 1179680 | tf_op jit(solution)/shard_map/ppermute | solution.py:79
  516.2 15.7 %collective-permute-done.12 = bf16[2,2,73728]{2,1,0:T(2,128)(2,1)S(1)} collective-permute-done((bf16[2,2,73728]{2,1,0:T(2,128)(2,1)S(1)}, bf16[2,2,73728]{2,1,0:T(2,128)(2,1)S(1)}, u32[]{:S(2)}, u32[]{:S(2)}) %collective-permute-start.12) | collective-permute-done | bytes 589856 | tf_op jit(solution)/shard_map/ppermute | solution.py:79
  532.8 11.3 %collective-permute-done.17 = bf16[2,2,73728]{2,1,0:T(2,128)(2,1)S(1)} collective-permute-done((bf16[2,2,73728]{2,1,0:T(2,128)(2,1)S(1)}, bf16[2,2,73728]{2,1,0:T(2,128)(2,1)S(1)}, u32[]{:S(2)}, u32[]{:S(2)}) %collective-permute-start.17) | collective-permute-done | bytes 589856 | tf_op jit(solution)/shard_map/ppermute | solution.py:79
  545.1 8.0 %collective-permute-done.13 = bf16[2,73728]{1,0:T(2,128)(2,1)S(1)} collective-permute-done((bf16[2,73728]{1,0:T(2,128)(2,1)S(1)}, bf16[2,73728]{1,0:T(2,128)(2,1)S(1)}, u32[]{:S(2)}, u32[]{:S(2)}) %collective-permute-start.13) | collective-permute-done | bytes 294944 | tf_op jit(solution)/shard_map/ppermute | solution.py:79
  555.3 3.3 collective-permute-done.18
  576.8 3.0 collective-permute-start.23
  (314 shorter events, 159.9 us)
Async XLA Ops:
  0.7 94.6 %copy-start = (bf16[768,768]{1,0:T(8,128)(2,1)S(1)}, bf16[768,768]{1,0:T(8,128)(2,1)}, u32[]{:S(2)}) copy-start(bf16[768,768]{1,0:T(8,128)(2,1)} %param.35) | copy-start | bytes 3538948
  0.7 24.5 %all-to-all-start = ((bf16[4,256,768]{2,1,0:T(8,128)(2,1)}), bf16[4,256,768]{2,1,0:T(8,128)(2,1)S(1)}, u32[]{:S(2)}, u32[]{:S(2)}) async-start(bf16[4,256,768]{2,1,0:T(8,128)(2,1)} %param.29), calls=%async_computation | async-start | bytes 3145728 | tf_op jit(solution)/shard_map/all_to_all | solution.py:145
  6.6 74.7 %copy-start.8 = (pred[2,512,512]{1,2,0:T(8,128)(4,1)}, pred[2,512,512]{1,2,0:T(8,128)(4,1)S(1)}, u32[]{:S(2)}) copy-start(pred[2,512,512]{1,2,0:T(8,128)(4,1)S(1)} %compare_or_fusion) | copy-start | bytes 1572868
  25.2 29.8 %all-to-all-start.2 = ((bf16[4,256,768]{2,1,0:T(8,128)(2,1)}), bf16[4,256,768]{2,1,0:T(8,128)(2,1)}, u32[]{:S(2)}, u32[]{:S(2)}) async-start(bf16[4,256,768]{2,1,0:T(8,128)(2,1)} %param.30), calls=%async_computation.2 | async-start | bytes 3145728 | tf_op jit(solution)/shard_map/all_to_all | solution.py:145
  55.0 14.5 %copy-start.4 = (bf16[2,512,12,64]{1,0,3,2:T(2,128)(2,1)}, bf16[2,512,12,64]{1,0,3,2:T(2,128)(2,1)S(1)}, u32[]{:S(2)}) copy-start(bf16[2,512,12,64]{1,0,3,2:T(2,128)(2,1)S(1)} %reshape_reshape.7) | copy-start | bytes 4718596
  69.5 11.8 %copy-start.11 = (bf16[2,512,12,64]{1,0,3,2:T(2,128)(2,1)S(1)}, bf16[2,512,12,64]{1,0,3,2:T(2,128)(2,1)}, u32[]{:S(2)}) copy-start(bf16[2,512,12,64]{1,0,3,2:T(2,128)(2,1)} %reshape_reshape.6) | copy-start | bytes 4718596
  95.4 38.3 %slice-start.4 = ((s8[4718592]{0:T(1024)(128)(4,1)}), s8[4194304]{0:T(1024)(128)(4,1)S(1)}, s32[]{:S(2)}) async-start(s8[4718592]{0:T(1024)(128)(4,1)} %bitcast.240), calls=%async_computation.8 | async-start | bytes 8388608
  97.6 36.0 %copy-start.44 = (f32[1024]{0:T(1024)}, f32[1024]{0:T(1024)S(1)}, u32[]{:S(2)}) copy-start(f32[1024]{0:T(1024)S(1)} %multiply_reduce_fusion.5) | copy-start | bytes 12292
  98.2 35.4 %copy-start.54 = (f32[768]{0:T(1024)S(1)}, f32[768]{0:T(1024)}, u32[]{:S(2)}) copy-start(f32[768]{0:T(1024)} %get-tuple-element.80) | copy-start | bytes 9220
  98.2 35.4 %slice-start.5 = ((s8[4718592]{0:T(1024)(128)(4,1)}), s8[524288]{0:T(1024)(128)(4,1)S(1)}, s32[]{:S(2)}) async-start(s8[4718592]{0:T(1024)(128)(4,1)} %bitcast.240), calls=%async_computation.9 | async-start | bytes 1048576
  203.2 13.0 %copy-start.12 = (bf16[2,512,12,64]{1,0,3,2:T(2,128)(2,1)S(1)}, bf16[2,512,12,64]{1,0,3,2:T(2,128)(2,1)}, u32[]{:S(2)}) copy-start(bf16[2,512,12,64]{1,0,3,2:T(2,128)(2,1)} %reshape_reshape.6) | copy-start | bytes 4718596
  234.3 21.9 %copy-start.7 = (bf16[2,512,12,64]{1,0,3,2:T(2,128)(2,1)S(1)}, bf16[2,512,12,64]{1,0,3,2:T(2,128)(2,1)}, u32[]{:S(2)}) copy-start(bf16[2,512,12,64]{1,0,3,2:T(2,128)(2,1)} %reshape.276) | copy-start | bytes 4718596
  284.4 121.6 %all-to-all-start.1 = ((bf16[2,512,768]{2,0,1:T(2,128)(2,1)}), bf16[2,512,768]{2,0,1:T(2,128)(2,1)S(1)}, u32[]{:S(2)}, u32[]{:S(2)}) async-start(bf16[2,512,768]{2,0,1:T(2,128)(2,1)} %copy.114), calls=%async_computation.1 | async-start | bytes 3145728 | tf_op jit(solution)/shard_map/all_to_all | solution.py:146
  316.7 62.5 %collective-permute-start.5 = (bf16[2,2,2,2,18432]{4,3,2,1,0:T(2,128)(2,1)}, bf16[2,2,2,2,18432]{4,3,2,1,0:T(2,128)(2,1)}, u32[]{:S(2)}, u32[]{:S(2)}) collective-permute-start(bf16[2,2,2,2,18432]{4,3,2,1,0:T(2,128)(2,1)} %dynamic-slice_bitcast_fusion.8), channel_id=1, source_target_pairs={{0,2},{1,3},{2,0},{3,1},{4,6},{5,7},{6,4},{7,5},{8,10},{9,11},{10,... | collective-permute-start | bytes 1769480 | tf_op jit(solution)/shard_map/ppermute | solution.py:79
  338.4 101.9 %collective-permute-start.15 = (bf16[2,2,2,2,73728]{4,3,2,1,0:T(2,128)(2,1)}, bf16[2,2,2,2,73728]{4,3,2,1,0:T(2,128)(2,1)}, u32[]{:S(2)}, u32[]{:S(2)}) collective-permute-start(bf16[2,2,2,2,73728]{4,3,2,1,0:T(2,128)(2,1)} %dynamic-slice_bitcast_fusion), channel_id=1, source_target_pairs={{0,2},{1,3},{2,0},{3,1},{4,6},{5,7},{6,4},{7,5},{8,10},{9,11},{10,... | collective-permute-start | bytes 7077896 | tf_op jit(solution)/shard_map/ppermute | solution.py:79
  338.9 126.6 %collective-permute-start.10 = (bf16[2,2,2,2,73728]{4,3,2,1,0:T(2,128)(2,1)}, bf16[2,2,2,2,73728]{4,3,2,1,0:T(2,128)(2,1)}, u32[]{:S(2)}, u32[]{:S(2)}) collective-permute-start(bf16[2,2,2,2,73728]{4,3,2,1,0:T(2,128)(2,1)} %dynamic-slice_bitcast_fusion.1), channel_id=1, source_target_pairs={{0,2},{1,3},{2,0},{3,1},{4,6},{5,7},{6,4},{7,5},{8,10},{9,11},{10,... | collective-permute-start | bytes 7077896 | tf_op jit(solution)/shard_map/ppermute | solution.py:79
  344.8 32.5 %collective-permute-start.25 = (f32[9216]{0:T(1024)S(1)}, f32[9216]{0:T(1024)S(1)}, u32[]{:S(2)}, u32[]{:S(2)}) collective-permute-start(f32[9216]{0:T(1024)S(1)} %constant_dynamic-update-slice_fusion), channel_id=1, source_target_pairs={{0,2},{1,3},{2,0},{3,1},{4,6},{5,7},{6,4},{7,5},{8,10},{9,11},{10,... | collective-permute-start | bytes 110600 | tf_op jit(solution)/shard_map/ppermute | solution.py:79
  377.3 8.4 %collective-permute-start.26 = (f32[9216]{0:T(1024)S(1)}, f32[9216]{0:T(1024)S(1)}, u32[]{:S(2)}, u32[]{:S(2)}) collective-permute-start(f32[9216]{0:T(1024)S(1)} %add.448), channel_id=1, source_target_pairs={{0,4},{1,5},{2,6},{3,7},{4,0},{5,1},{6,2},{7,3},{8,12},{9,13},{10,... | collective-permute-start | bytes 110600 | tf_op jit(solution)/shard_map/ppermute | solution.py:79
  381.0 11.1 %copy-start.23 = (bf16[96,8,2,512]{3,1,2,0:T(8,128)(2,1)S(1)}, bf16[96,8,2,512]{3,1,2,0:T(8,128)(2,1)}, u32[]{:S(2)}) copy-start(bf16[96,8,2,512]{3,1,2,0:T(8,128)(2,1)} %copy-done.22) | copy-start | bytes 4718596
  381.3 8.7 %collective-permute-start.6 = (bf16[2,2,2,18432]{3,2,1,0:T(2,128)(2,1)S(1)}, bf16[2,2,2,18432]{3,2,1,0:T(2,128)(2,1)S(1)}, u32[]{:S(2)}, u32[]{:S(2)}) collective-permute-start(bf16[2,2,2,18432]{3,2,1,0:T(2,128)(2,1)S(1)} %dynamic-slice_bitcast_fusion.12), channel_id=1, source_target_pairs={{0,4},{1,5},{2,6},{3,7},{4,0},{5,1},{6,2},{7,3},{8,12},{9,13},{10,... | collective-permute-start | bytes 884744 | tf_op jit(solution)/shard_map/ppermute | solution.py:79
  385.8 7.8 %collective-permute-start.27 = (f32[9216]{0:T(1024)S(1)}, f32[9216]{0:T(1024)S(1)}, u32[]{:S(2)}, u32[]{:S(2)}) collective-permute-start(f32[9216]{0:T(1024)S(1)} %add.449), channel_id=1, source_target_pairs={{0,8},{1,9},{2,10},{3,11},{4,12},{5,13},{6,14},{7,15},{8,0},{9,1},... | collective-permute-start | bytes 110600 | tf_op jit(solution)/shard_map/ppermute | solution.py:79
  390.5 5.8 collective-permute-start.7
  393.6 10.3 %collective-permute-start.28 = (f32[9216]{0:T(1024)S(1)}, f32[9216]{0:T(1024)S(1)}, u32[]{:S(2)}, u32[]{:S(2)}) collective-permute-start(f32[9216]{0:T(1024)S(1)} %add.450), channel_id=1, source_target_pairs={{0,16},{1,17},{2,18},{3,19},{4,20},{5,21},{6,22},{7,23},{8,24},{9,... | collective-permute-start | bytes 110600 | tf_op jit(solution)/shard_map/ppermute | solution.py:79
  397.1 14.1 %collective-permute-start.8 = (bf16[2,18432]{1,0:T(2,128)(2,1)}, bf16[2,18432]{1,0:T(2,128)(2,1)S(1)}, u32[]{:S(2)}, u32[]{:S(2)}) collective-permute-start(bf16[2,18432]{1,0:T(2,128)(2,1)} %dynamic-slice_bitcast_fusion.15), channel_id=1, source_target_pairs={{0,16},{1,17},{2,18},{3,19},{4,20},{5,21},{6,22},{7,23},{8,24},{9,... | collective-permute-start | bytes 221192 | tf_op jit(solution)/shard_map/ppermute | solution.py:79
  403.9 31.1 %collective-permute-start = (bf16[2,2,2,2,55296]{4,3,2,1,0:T(2,128)(2,1)}, bf16[2,2,2,2,55296]{4,3,2,1,0:T(2,128)(2,1)}, u32[]{:S(2)}, u32[]{:S(2)}) collective-permute-start(bf16[2,2,2,2,55296]{4,3,2,1,0:T(2,128)(2,1)} %dynamic-slice_bitcast_fusion.2), channel_id=1, source_target_pairs={{0,2},{1,3},{2,0},{3,1},{4,6},{5,7},{6,4},{7,5},{8,10},{9,11},{10,... | collective-permute-start | bytes 5308424 | tf_op jit(solution)/shard_map/ppermute | solution.py:79
  404.0 9.7 %collective-permute-start.29 = (f32[9216]{0:T(1024)S(1)}, f32[9216]{0:T(1024)}, u32[]{:S(2)}, u32[]{:S(2)}) collective-permute-start(f32[9216]{0:T(1024)S(1)} %add.451), channel_id=1, source_target_pairs={{0,1},{1,0},{2,3},{3,2},{4,5},{5,4},{6,7},{7,6},{8,9},{9,8},{10,11... | collective-permute-start | bytes 110600 | tf_op jit(solution)/shard_map/ppermute | solution.py:79
  406.0 34.2 %slice-start.2 = ((s8[4718592]{0:T(1024)(128)(4,1)}), s8[524288]{0:T(1024)(128)(4,1)S(1)}, s32[]{:S(2)}) async-start(s8[4718592]{0:T(1024)(128)(4,1)} %bitcast.205), calls=%async_computation.6 | async-start | bytes 1048576
  406.0 25.5 %all-to-all-start.3 = ((bf16[2,512,768]{2,0,1:T(2,128)(2,1)}), bf16[2,512,768]{2,0,1:T(2,128)(2,1)}, u32[]{:S(2)}, u32[]{:S(2)}) async-start(bf16[2,512,768]{2,0,1:T(2,128)(2,1)} %copy.129), calls=%async_computation.3 | async-start | bytes 3145728 | tf_op jit(solution)/shard_map/all_to_all | solution.py:146
  411.6 22.9 %collective-permute-start.9 = (bf16[18432]{0:T(1024)(128)(2,1)S(1)}, bf16[18432]{0:T(1024)(128)(2,1)S(1)}, u32[]{:S(2)}, u32[]{:S(2)}) collective-permute-start(bf16[18432]{0:T(1024)(128)(2,1)S(1)} %get-tuple-element.77), channel_id=1, source_target_pairs={{0,1},{1,0},{2,3},{3,2},{4,5},{5,4},{6,7},{7,6},{8,9},{9,8},{10,11... | collective-permute-start | bytes 110600 | tf_op jit(solution)/shard_map/ppermute | solution.py:79
  438.9 26.6 %slice-start = ((s8[4718592]{0:T(1024)(128)(4,1)}), s8[4194304]{0:T(1024)(128)(4,1)S(1)}, s32[]{:S(2)}) async-start(s8[4718592]{0:T(1024)(128)(4,1)} %bitcast.203), calls=%async_computation.4 | async-start | bytes 8388608
  439.5 25.9 %slice-start.1 = ((s8[4718592]{0:T(1024)(128)(4,1)}), s8[524288]{0:T(1024)(128)(4,1)S(1)}, s32[]{:S(2)}) async-start(s8[4718592]{0:T(1024)(128)(4,1)} %bitcast.203), calls=%async_computation.5 | async-start | bytes 1048576
  439.5 22.6 %collective-permute-start.1 = (bf16[2,2,2,55296]{3,2,1,0:T(2,128)(2,1)S(1)}, bf16[2,2,2,55296]{3,2,1,0:T(2,128)(2,1)S(1)}, u32[]{:S(2)}, u32[]{:S(2)}) collective-permute-start(bf16[2,2,2,55296]{3,2,1,0:T(2,128)(2,1)S(1)} %dynamic-slice_bitcast_fusion.5), channel_id=1, source_target_pairs={{0,4},{1,5},{2,6},{3,7},{4,0},{5,1},{6,2},{7,3},{8,12},{9,13},{10,... | collective-permute-start | bytes 2654216 | tf_op jit(solution)/shard_map/ppermute | solution.py:79
  445.2 69.2 %collective-permute-start.16 = (bf16[2,2,2,73728]{3,2,1,0:T(2,128)(2,1)S(1)}, bf16[2,2,2,73728]{3,2,1,0:T(2,128)(2,1)S(1)}, u32[]{:S(2)}, u32[]{:S(2)}) collective-permute-start(bf16[2,2,2,73728]{3,2,1,0:T(2,128)(2,1)S(1)} %dynamic-slice_bitcast_fusion.3), channel_id=1, source_target_pairs={{0,4},{1,5},{2,6},{3,7},{4,0},{5,1},{6,2},{7,3},{8,12},{9,13},{10,... | collective-permute-start | bytes 3538952 | tf_op jit(solution)/shard_map/ppermute | solution.py:79
  463.4 10.2 %collective-permute-start.2 = (bf16[2,2,55296]{2,1,0:T(2,128)(2,1)S(1)}, bf16[2,2,55296]{2,1,0:T(2,128)(2,1)S(1)}, u32[]{:S(2)}, u32[]{:S(2)}) collective-permute-start(bf16[2,2,55296]{2,1,0:T(2,128)(2,1)S(1)} %dynamic-slice_bitcast_fusion.9), channel_id=1, source_target_pairs={{0,8},{1,9},{2,10},{3,11},{4,12},{5,13},{6,14},{7,15},{8,0},{9,1},... | collective-permute-start | bytes 1327112 | tf_op jit(solution)/shard_map/ppermute | solution.py:79
  474.3 9.3 %collective-permute-start.3 = (bf16[2,55296]{1,0:T(2,128)(2,1)S(1)}, bf16[2,55296]{1,0:T(2,128)(2,1)S(1)}, u32[]{:S(2)}, u32[]{:S(2)}) collective-permute-start(bf16[2,55296]{1,0:T(2,128)(2,1)S(1)} %dynamic-slice_bitcast_fusion.13), channel_id=1, source_target_pairs={{0,16},{1,17},{2,18},{3,19},{4,20},{5,21},{6,22},{7,23},{8,24},{9,... | collective-permute-start | bytes 663560 | tf_op jit(solution)/shard_map/ppermute | solution.py:79
  475.4 35.4 %collective-permute-start.11 = (bf16[2,2,2,73728]{3,2,1,0:T(2,128)(2,1)S(1)}, bf16[2,2,2,73728]{3,2,1,0:T(2,128)(2,1)S(1)}, u32[]{:S(2)}, u32[]{:S(2)}) collective-permute-start(bf16[2,2,2,73728]{3,2,1,0:T(2,128)(2,1)S(1)} %dynamic-slice_bitcast_fusion.4), channel_id=1, source_target_pairs={{0,4},{1,5},{2,6},{3,7},{4,0},{5,1},{6,2},{7,3},{8,12},{9,13},{10,... | collective-permute-start | bytes 3538952 | tf_op jit(solution)/shard_map/ppermute | solution.py:79
  484.6 76.5 %collective-permute-start.4 = (bf16[55296]{0:T(1024)(128)(2,1)S(1)}, bf16[55296]{0:T(1024)(128)(2,1)S(1)}, u32[]{:S(2)}, u32[]{:S(2)}) collective-permute-start(bf16[55296]{0:T(1024)(128)(2,1)S(1)} %get-tuple-element.75), channel_id=1, source_target_pairs={{0,1},{1,0},{2,3},{3,2},{4,5},{5,4},{6,7},{7,6},{8,9},{9,8},{10,11... | collective-permute-start | bytes 331784 | tf_op jit(solution)/shard_map/ppermute | solution.py:79
  512.4 19.5 %collective-permute-start.12 = (bf16[2,2,73728]{2,1,0:T(2,128)(2,1)S(1)}, bf16[2,2,73728]{2,1,0:T(2,128)(2,1)S(1)}, u32[]{:S(2)}, u32[]{:S(2)}) collective-permute-start(bf16[2,2,73728]{2,1,0:T(2,128)(2,1)S(1)} %dynamic-slice_bitcast_fusion.7), channel_id=1, source_target_pairs={{0,8},{1,9},{2,10},{3,11},{4,12},{5,13},{6,14},{7,15},{8,0},{9,1},... | collective-permute-start | bytes 1769480 | tf_op jit(solution)/shard_map/ppermute | solution.py:79
  516.1 28.1 %collective-permute-start.17 = (bf16[2,2,73728]{2,1,0:T(2,128)(2,1)S(1)}, bf16[2,2,73728]{2,1,0:T(2,128)(2,1)S(1)}, u32[]{:S(2)}, u32[]{:S(2)}) collective-permute-start(bf16[2,2,73728]{2,1,0:T(2,128)(2,1)S(1)} %dynamic-slice_bitcast_fusion.6), channel_id=1, source_target_pairs={{0,8},{1,9},{2,10},{3,11},{4,12},{5,13},{6,14},{7,15},{8,0},{9,1},... | collective-permute-start | bytes 1769480 | tf_op jit(solution)/shard_map/ppermute | solution.py:79
  532.7 20.4 %collective-permute-start.13 = (bf16[2,73728]{1,0:T(2,128)(2,1)S(1)}, bf16[2,73728]{1,0:T(2,128)(2,1)S(1)}, u32[]{:S(2)}, u32[]{:S(2)}) collective-permute-start(bf16[2,73728]{1,0:T(2,128)(2,1)S(1)} %dynamic-slice_bitcast_fusion.11), channel_id=1, source_target_pairs={{0,16},{1,17},{2,18},{3,19},{4,20},{5,21},{6,22},{7,23},{8,24},{9,... | collective-permute-start | bytes 884744 | tf_op jit(solution)/shard_map/ppermute | solution.py:79
  545.0 13.7 %collective-permute-start.18 = (bf16[2,73728]{1,0:T(2,128)(2,1)S(1)}, bf16[2,73728]{1,0:T(2,128)(2,1)S(1)}, u32[]{:S(2)}, u32[]{:S(2)}) collective-permute-start(bf16[2,73728]{1,0:T(2,128)(2,1)S(1)} %dynamic-slice_bitcast_fusion.10), channel_id=1, source_target_pairs={{0,16},{1,17},{2,18},{3,19},{4,20},{5,21},{6,22},{7,23},{8,24},{9,... | collective-permute-start | bytes 884744 | tf_op jit(solution)/shard_map/ppermute | solution.py:79
  554.5 8.5 %collective-permute-start.14 = (bf16[73728]{0:T(1024)(128)(2,1)S(1)}, bf16[73728]{0:T(1024)(128)(2,1)S(1)}, u32[]{:S(2)}, u32[]{:S(2)}) collective-permute-start(bf16[73728]{0:T(1024)(128)(2,1)S(1)} %get-tuple-element.73), channel_id=1, source_target_pairs={{0,1},{1,0},{2,3},{3,2},{4,5},{5,4},{6,7},{7,6},{8,9},{9,8},{10,11... | collective-permute-start | bytes 442376 | tf_op jit(solution)/shard_map/ppermute | solution.py:79
  560.1 5.2 collective-permute-start.19
  566.6 1.2 collective-permute-start.20
  568.4 3.6 collective-permute-start.21
  572.6 3.6 collective-permute-start.22
  576.8 4.5 collective-permute-start.23
  581.9 3.6 collective-permute-start.24
  (53 other events, 270.8 us)

commit v2 on v1

v2 whole, which is shorter than its diff:
```python
import functools
import math

import jax
import jax.numpy as jnp
from jax import lax
from jax.experimental import pallas as pl
from jax.experimental.pallas import tpu as pltpu
from jax.sharding import PartitionSpec as P

HD = 64
STEP = 10
EPS_NORM = 1e-06
NEG_BIG = -1e30
BETA_ONE = 0.9
BETA_TWO = 0.999
ADAM_EPS = 1e-08
DECAY = 0.01
EMA_KEEP = 0.8
SMALL_RATE = 0.1
AXES = ("batch", "seq")
MESH = pl.DeviceIdType.MESH
VMEM_BYTES = 61 << 20
BF = jnp.bfloat16
F32 = jnp.float32


def nn(left, right):
    return lax.dot_general(left, right, (((1,), (0,)), ((), ())), preferred_element_type=F32)


def nt(left, right):
    return lax.dot_general(left, right, (((1,), (1,)), ((), ())), preferred_element_type=F32)


def tn(left, right):
    return lax.dot_general(left, right, (((0,), (0,)), ((), ())), preferred_element_type=F32)


def row_mean(values):
    return jnp.mean(values, axis=1, keepdims=True)


def column_sum(values):
    return jnp.sum(values, axis=0, keepdims=True)


def gelu_pair(inner):
    size = jnp.abs(inner) * 0.7071067811865476
    t = 1.0 / (1.0 + 0.3275911 * size)
    bell = jnp.exp(inner * inner * -0.5)
    series = (((1.061405429 * t - 1.453152027) * t + 1.421413741) * t - 0.284496736) * t
    half = (series + 0.254829592) * t * (0.5 * bell)
    share = jnp.where(inner > 0, 1.0 - half, half)
    return inner * share, share + inner * bell * 0.3989422804014327


def small_row(packed, index, width):
    lines = width // 128
    return jnp.concatenate([packed[index * lines + i : index * lines + i + 1, :] for i in range(lines)], axis=1)


def head_masks():
    lane = lax.broadcasted_iota(jnp.int32, (1, 2 * HD), 1)
    return (lane < HD, lane >= HD)


def forward_kernel(
    tables_h, cot_h, seg_h, row_h, col_h, wqkv_h, wo_h, w1_h, w2_h, small_h,
    x_o, q_o, k_o, v_o, e_o, rinv_o, ctx_o, h1_o, xh_o, rstd_o, a_o, g_o, dr2_o, lo_o, sg_o,
    x, cot, seg, row, col, wqkv, wo, w1, w2, small, bias, inner_bias,
    q, k, v, e, rinv, ctx, h1, xh, rstd, a, g, dr2, lo, sg, h1f,
    in_sem, out_sem, e_sem, send_sem, recv_sem,
):
    tabs, length, width = x.shape
    block = length // 2
    hidden = w1.shape[1]
    pairs = width // (2 * HD)
    batch, me = lax.axis_index("batch"), lax.axis_index("seq")
    peer = (batch, 1 - me)
    copy = pltpu.make_async_copy
    barrier = pltpu.get_barrier_semaphore()
    pl.semaphore_signal(barrier, inc=1, device_id=peer, device_id_type=MESH)
    own_rows = pl.ds(pl.multiple_of(me * block, block), block)
    peer_rows = pl.ds(pl.multiple_of((1 - me) * block, block), block)

    sources = [(small_h, small), (wqkv_h, wqkv), (seg_h, seg), (row_h, row), (col_h, col)]
    sources += [(wo_h, wo), (w1_h, w1), (w2_h, w2)]
    sources += [(tables_h.at[me * tabs + t], x.at[t, own_rows]) for t in range(tabs)]
    sources += [(cot_h.at[me * tabs + t], cot.at[t, own_rows]) for t in range(tabs)]
    loads = [copy(src, dst, in_sem.at[i]) for i, (src, dst) in enumerate(sources)]
    for i in (8, 9, 1, 0, 2, 3, 4, 5, 6, 7, 10, 11):
        loads[i].start()

    def swap(index):
        source, place = (tables_h, x) if index < tabs else (cot_h, cot)
        t = index % tabs
        return pltpu.make_async_remote_copy(
            src_ref=source.at[(1 - me) * tabs + t],
            dst_ref=place.at[t, own_rows],
            send_sem=send_sem.at[index],
            recv_sem=recv_sem.at[index],
            device_id=peer,
            device_id_type=MESH,
        )

    pl.semaphore_wait(barrier, 1)
    for index in range(2 * tabs):
        swap(index).start()

    stores = []

    def store(index, src, dst):
        stores.append(copy(src, dst, out_sem.at[index]))
        stores[-1].start()

    for i in (0, 1, 8, 9):
        loads[i].wait()
    gain1, gain2, shift1, shift2, bias_q, bias_v, bias_o, bias_f2 = (
        small_row(small, i, width) for i in range(8)
    )
    inner_bias[...] = small_row(small[8 * (width // 128) :, :], 0, hidden)
    masks = head_masks()
    zero = jnp.zeros((), BF)

    def project(t, rows):
        block_x = x[t, rows, :]
        q[t, rows, :] = ((nn(block_x, wqkv[0]) + bias_q) * (HD**-0.5)).astype(BF)
        k[t, rows, :] = nn(block_x, wqkv[1]).astype(BF)
        v[t, rows, :] = (nn(block_x, wqkv[2]) + bias_v).astype(BF)

    for t in range(tabs):
        project(t, own_rows)
    for i in (2, 3, 4):
        loads[i].wait()
    for t in range(tabs):
        keys = [ids[pl.ds(me * tabs + t, 1), :].astype(F32) for ids in (seg, row, col)]
        wide = [jnp.transpose(jnp.broadcast_to(ids, (128, length)))[:, 0:1] for ids in keys]
        seen = (wide[0] == 0.0) | (keys[0] == 0.0)
        seen = seen | (wide[1] == keys[1]) | (wide[2] == keys[2])
        bias[t] = jnp.where(seen, 0.0, NEG_BIG).astype(BF)

    for t in range(tabs):
        swap(t).wait_recv()
        project(t, peer_rows)
        store(16 * t + 14, x.at[t], x_o.at[t])

        def pair(hp, carry):
            lanes = pl.ds(pl.multiple_of(hp * 2 * HD, 2 * HD), 2 * HD)
            slot = lax.rem(hp, 2)

            @pl.when(t * pairs + hp >= 2)
            def _():
                copy(e.at[slot], e_o.at[0, 0], e_sem.at[slot]).wait()

            q2, k2, v2 = q[t, :, lanes], k[t, :, lanes], v[t, :, lanes]
            one = jnp.ones((length, 2 * HD), BF)
            off = bias[t].astype(F32)
            for h in range(2):
                scores = nt(jnp.where(masks[h], q2, zero), k2) + off
                top = jnp.max(scores, axis=1, keepdims=True)
                e[slot, :, h * length : (h + 1) * length] = jnp.exp(scores - top).astype(BF)
            right = [
                jnp.concatenate([jnp.where(m, v2, zero), jnp.where(m, one, zero)], axis=1)
                for m in masks
            ]
            both = nn(e[slot], jnp.concatenate(right, axis=0))
            inverse = 1.0 / both[:, 2 * HD :]
            rinv[t, :, lanes] = inverse.astype(BF)
            ctx[t, :, lanes] = (both[:, : 2 * HD] * inverse).astype(BF)
            copy(e.at[slot], e_o.at[t, hp], e_sem.at[slot]).start()
            return carry

        lax.fori_loop(0, pairs, pair, 0)
        for i, (src, dst) in enumerate(((q, q_o), (k, k_o), (v, v_o), (rinv, rinv_o), (ctx, ctx_o))):
            store(16 * t + i, src.at[t], dst.at[t])
        if t == 0:
            loads[5].wait()
        sum1 = x[t].astype(F32) + nn(ctx[t], wo[...]) + bias_o
        centre = sum1 - row_mean(sum1)
        scale = lax.rsqrt(row_mean(centre * centre) + EPS_NORM)
        unit = centre * scale
        xh[t] = unit.astype(BF)
        rstd[t] = jnp.broadcast_to(scale, (length, 128))
        normed = unit * gain1 + shift1
        h1f[...] = normed
        h1[t] = normed.astype(BF)
        for i, (src, dst) in enumerate(((h1, h1_o), (xh, xh_o), (rstd, rstd_o))):
            store(16 * t + 5 + i, src.at[t], dst.at[t])
        if t == 0:
            loads[6].wait()
        rows = pl.ds(t * length, length)
        step = 256

        def inner(j, carry):
            for sub in range(width // step):
                here = slice(sub * step, (sub + 1) * step)
                there = pl.ds(pl.multiple_of(j * width + sub * step, step), step)
                active, slope = gelu_pair(nn(h1[t], w1[:, there]) + inner_bias[0:1, there])
                a[j, rows, here] = active.astype(BF)
                g[j, rows, here] = slope.astype(BF)
            return carry

        lax.fori_loop(0, hidden // width, inner, 0)
        store(16 * t + 8, a.at[:, rows], a_o.at[:, rows])
        store(16 * t + 9, g.at[:, rows], g_o.at[:, rows])
        if t == 0:
            loads[7].wait()
        sum2 = h1f[...] + bias_f2
        for j in range(hidden // width):
            sum2 = sum2 + nn(a[j, rows, :], w2[j * width : (j + 1) * width, :])
        centre = sum2 - row_mean(sum2)
        scale = lax.rsqrt(row_mean(centre * centre) + EPS_NORM)
        unit = centre * scale
        lo[t] = (unit * gain2 + shift2).astype(BF)
        loads[10 + t].wait()
        swap(tabs + t).wait_recv()
        back = cot[t].astype(F32)
        d_unit = back * gain2
        d_sum2 = scale * (d_unit - row_mean(d_unit) - unit * row_mean(d_unit * unit))
        dr2[t] = d_sum2
        parts = [column_sum(back * unit), column_sum(back), column_sum(d_sum2.astype(BF).astype(F32))]
        parts = jnp.concatenate(parts + [jnp.zeros((5, width), F32)], axis=0)
        sg[...] = parts if t == 0 else sg[...] + parts
        store(16 * t + 10, dr2.at[t], dr2_o.at[t])
        store(16 * t + 11, lo.at[t], lo_o.at[t])
    store(12, sg, sg_o)
    for stored in stores:
        stored.wait()
    for slot in range(2):
        copy(e.at[slot], e_o.at[0, 0], e_sem.at[slot]).wait()
    for index in range(2 * tabs):
        swap(index).wait_send()


def anywhere(count):
    return [pl.BlockSpec(memory_space=pl.ANY)] * count


def forward(tables_in, out_cot, seg, row, col, wqkv, wo, w1, w2, small):
    tabs, length = tables_in.shape[0] // 2, tables_in.shape[1] * 2
    width, hidden = w1.shape
    pairs, chunks, rows = width // (2 * HD), hidden // width, tabs * length
    shape = jax.ShapeDtypeStruct
    act = shape((tabs, length, width), BF)
    wide = shape((chunks, rows, width), BF)
    outs = [act] * 4 + [shape((tabs, pairs, length, 2 * length), BF)] + [act] * 4
    outs += [shape((tabs, length, 128), F32), wide, wide, shape(act.shape, F32), act]
    outs += [shape((8, width), F32)]
    ins = (tables_in, out_cot, seg, row, col, wqkv, wo, w1, w2, small)
    like = lambda array: pltpu.VMEM(array.shape, array.dtype)
    scratch = [like(act), like(act)] + [like(array) for array in ins[2:]]
    scratch += [pltpu.VMEM((tabs, length, length), BF), pltpu.VMEM((1, hidden), F32)]
    scratch += [like(array) for array in outs[1:4]] + [pltpu.VMEM((2, length, 2 * length), BF)]
    scratch += [like(array) for array in outs[5:]] + [pltpu.VMEM((length, width), F32)]
    dma = pltpu.SemaphoreType.DMA
    return pl.pallas_call(
        forward_kernel,
        out_shape=outs,
        in_specs=anywhere(len(ins)),
        out_specs=anywhere(len(outs)),
        scratch_shapes=scratch + [dma((16,)), dma((16 * tabs,)), dma((2,)), dma((8,)), dma((8,))],
        compiler_params=pltpu.CompilerParams(
            vmem_limit_bytes=VMEM_BYTES, collective_id=0, has_side_effects=True
        ),
        name="layer_forward",
    )(*ins)


class Link:
    FIRST_Y = ("core", "y", "z", "w", "x")
    FIRST_Z = ("core", "z", "w", "y", "x")

    def __init__(self, rest, g2, g1, full, sm, grad, lo_h, outs):
        (self.half2, self.z2, self.w2, self.y2, self.x2, self.half, self.two, self.one, self.last) = rest[:9]
        (self.x_send, self.x_get, self.final2, self.final, self.slots8, self.slots4) = rest[9:15]
        (self.square8, self.square4, self.send_sem, self.recv_sem, self.own_sem) = rest[15:]
        self.g2, self.g1, self.full, self.sm, self.grad = g2, g1, full, sm, grad
        self.lo_h, self.outs = lo_h, outs
        batch, seq = lax.axis_index("batch"), lax.axis_index("seq")
        self.batch, self.seq = batch, seq
        self.bit = {
            "core": lax.rem(batch, 2),
            "y": lax.rem(batch // 2, 2),
            "z": lax.rem(batch // 4, 2),
            "w": batch // 8,
            "x": seq,
        }
        self.jump = {"core": 1, "y": 2, "z": 4, "w": 8}
        count = g1.shape[0] + 4
        self.state = [0] * count
        self.memo = None
        self.order = [self.FIRST_Y] * count
        self.held = [["w", "z", "y"] for _ in range(count)]
        self.near = [None] + [tuple(n for b, n in ((1, "x"), (2, "core"), (4, "y")) if m & b) for m in range(1, 8)]
        self.far = [None] + [tuple(n for b, n in ((1, "z"), (2, "w")) if m & b) for m in range(1, 4)]

    def device(self, names):
        batch, seq = self.batch, self.seq
        for name in names:
            if name == "x":
                seq = 1 - seq
            else:
                batch = batch + self.jump[name] * (1 - 2 * self.bit[name])
        return (batch, seq)

    def remote(self, index, src, dst, names):
        return pltpu.make_async_remote_copy(
            src_ref=src,
            dst_ref=dst,
            send_sem=self.send_sem.at[index],
            recv_sem=self.recv_sem.at[index],
            device_id=self.device(names),
            device_id_type=MESH,
        )

    def source(self, chunk):
        kept = self.g1.shape[0]
        other = 1 - self.bit["core"]
        if chunk < kept:
            return self.g1.at[chunk, :, :, :, other]
        return self.full.at[(chunk + 3) % 4, :, :, :, other, pl.ds(0, self.g1.shape[-2])]

    def own(self, chunk):
        kept = self.g1.shape[0]
        core = self.bit["core"]
        if chunk < kept:
            return self.g1[chunk, :, :, :, core]
        return self.full[(chunk + 3) % 4, :, :, :, core, 0 : self.g1.shape[-2]]

    def pick(self, chunk, name, other):
        value = 1 - self.bit[name] if other else self.bit[name]
        return tuple(value if axis == name else slice(None) for axis in self.held[chunk])

    def phase(self, chunk, number):
        name = self.order[chunk][number]
        index = chunk * 5 + number
        if name == "core":
            return self.remote(index, self.source(chunk), self.half.at[chunk], (name,))
        if name == "x":
            return self.remote(index, self.x_send.at[chunk], self.x_get.at[chunk], (name,))
        stages = [self.half, self.two, self.one, self.last]
        src = stages[number - 1].at[(chunk,) + self.pick(chunk, name, True)]
        return self.remote(index, src, stages[number].at[chunk], (name,))

    def begin(self, chunk):
        self.phase(chunk, 0).start()

    def advance(self, *chunks):
        for chunk in chunks:
            number = self.state[chunk]
            name = self.order[chunk][number]
            stages = [self.half, self.two, self.one, self.last]
            self.phase(chunk, number).wait_recv()
            if name == "x":
                rows = self.final.shape[1]
                total = self.final[chunk] + self.x_get[chunk].astype(F32)[0:rows]
                self.final[chunk] = total
                self.state[chunk] = 5
                continue
            if name == "core":
                kept = self.own(chunk)
            else:
                kept = stages[number - 1][(chunk,) + self.pick(chunk, name, False)]
                self.held[chunk].remove(name)
            total = stages[number][chunk].astype(F32) + kept.astype(F32)
            if number < 3:
                stages[number][chunk] = total.astype(BF)
            else:
                rows = total.shape[0] // 2
                low, high = total[0:rows], total[rows:]
                upper = self.seq == 1
                self.final[chunk] = jnp.where(upper, high, low)
                pad = jnp.zeros((self.x_send.shape[1] - rows, low.shape[1]), F32)
                gone = jnp.concatenate([jnp.where(upper, low, high), pad], axis=0)
                self.x_send[chunk] = gone.astype(BF)
            self.state[chunk] = number + 1
            self.phase(chunk, number + 1).start()

    def core2(self, j):
        src = self.g2.at[j, :, 1 - self.bit["core"]]
        return self.remote(40 + j, src, self.half2.at[j // 2, j % 2], ("core",))

    def core2_done(self, *which):
        for j in which:
            self.core2(j).wait_recv()
            kept = self.g2[j, :, self.bit["core"]].astype(F32)
            self.half2[j // 2, j % 2] = (self.half2[j // 2, j % 2].astype(F32) + kept).astype(BF)

    def copy_z2(self, y):
        src = self.half2.at[:, 1 - self.bit["z"], y]
        return self.remote(44 + y, src, self.z2.at[y], ("z",))

    def copy_w2(self, y):
        return self.remote(46 + y, self.z2.at[y, 1 - self.bit["w"]], self.w2.at[y], ("w",))

    def copy_y2(self):
        return self.remote(48, self.w2.at[1 - self.bit["y"]], self.y2, ("y",))

    def copy_x2(self):
        rows = self.x2.shape[0]
        there = pl.ds(pl.multiple_of((1 - self.seq) * rows, rows), rows)
        return self.remote(49, self.y2.at[there], self.x2, ("x",))

    def z2_done(self, y):
        self.copy_z2(y).wait_recv()
        kept = self.half2[:, self.bit["z"], y].astype(F32)
        self.z2[y] = (self.z2[y].astype(F32) + kept).astype(BF)
        self.copy_w2(y).start()

    def w2_done(self, y):
        self.copy_w2(y).wait_recv()
        kept = self.z2[y, self.bit["w"]].astype(F32)
        self.w2[y] = (self.w2[y].astype(F32) + kept).astype(BF)

    def y2_done(self):
        self.copy_y2().wait_recv()
        kept = self.w2[self.bit["y"]].astype(F32)
        self.y2[...] = (self.y2[...].astype(F32) + kept).astype(BF)
        self.copy_x2().start()

    def x2_done(self):
        self.copy_x2().wait_recv()
        rows = self.x2.shape[0]
        here = pl.ds(pl.multiple_of(self.seq * rows, rows), rows)
        self.final2[...] = self.y2[here, :].astype(F32) + self.x2[...].astype(F32)

    def back(self, index, src, table, tabs):
        block = self.outs[0].shape[1]
        there = pl.ds(pl.multiple_of((1 - self.seq) * block, block), block)
        dst = self.outs[1 if index == 50 else 0]
        if index == 50:
            return self.remote(50, src.at[:, there], dst.at[pl.ds(self.seq * tabs, tabs)], ("x",))
        rows = pl.ds(pl.multiple_of(table * 2 * block + (1 - self.seq) * block, block), block)
        return self.remote(index, src.at[rows], dst.at[self.seq * tabs + table], ("x",))

    def keep(self, index, src, table, tabs):
        block = self.outs[0].shape[1]
        sem = self.own_sem.at[index - 50]
        dst = self.outs[1 if index == 50 else 0]
        here = pl.ds(pl.multiple_of(self.seq * block, block), block)
        if index == 50:
            return pltpu.make_async_copy(src.at[:, here], dst.at[pl.ds(self.seq * tabs, tabs)], sem)
        rows = pl.ds(pl.multiple_of(table * 2 * block + self.seq * block, block), block)
        return pltpu.make_async_copy(src.at[rows], dst.at[self.seq * tabs + table], sem)

    def spread(self, base, slots, groups):
        return [
            self.remote(base + m, slots.at[0], slots.at[m], groups[m])
            for m in range(1, len(groups))
        ]

    def gathered(self, base, slots, groups):
        for sent in self.spread(base, slots, groups):
            sent.wait_recv()
        terms = [slots[m] for m in range(len(groups))]
        while len(terms) > 1:
            terms = [terms[i] + terms[i + 1] for i in range(0, len(terms), 2)]
        return terms[0]

    def quiet(self, act):
        act()

    def start_all(self, copies):
        for each in copies:
            each.start()

    def at(self, name, n=None):
        tabs = self.lo_h.shape[0]
        if name == "enter":
            barrier = pltpu.get_barrier_semaphore()
            for names in self.near[1:] + self.far[1:]:
                pl.semaphore_signal(barrier, inc=1, device_id=self.device(names), device_id_type=MESH)
        elif name == "outer":
            if n == 0:
                pl.semaphore_wait(pltpu.get_barrier_semaphore(), len(self.near) + len(self.far) - 2)
            self.core2(n).start()
            if n == 0:
                self.back(50, self.lo_h, 0, tabs).start()
                self.keep(50, self.lo_h, 0, tabs).start()
        elif name == "slope":
            if n == 0:
                self.core2_done(0, 1)
            if n == 1:
                self.core2_done(2, 3)
                for y in range(2):
                    self.copy_z2(y).start()
        elif name == "inner":
            self.begin(n)
            if n:
                self.advance(n - 1)
        elif name == "norm":
            if n == 0:
                self.advance(3)
            else:
                self.z2_done(0)
                self.advance(0)
        elif name == "attn":
            self.begin(4)
        elif name == "context":
            self.advance(4, 1, 0)
        elif name == "attend":
            plan = {
                1: lambda: self.z2_done(1),
                3: lambda: (self.begin(5), self.advance(2, 1, 0)),
                4: lambda: self.advance(5),
                6: lambda: (self.w2_done(0), self.advance(3, 2, 1)),
                7: lambda: self.begin(6),
                8: lambda: self.advance(6, 0),
                9: lambda: (self.w2_done(1), self.copy_y2().start(), self.advance(4, 3, 2)),
                11: lambda: self.begin(7),
            }
            if self.memo is None:
                self.memo = (list(self.state), [list(held) for held in self.held])
            self.state, self.held = list(self.memo[0]), [list(held) for held in self.memo[1]]
            for k, act in plan.items():
                pl.when(n == k)(functools.partial(self.quiet, act))
        elif name == "attended":
            self.slots8[0] = self.sm[...]
            self.start_all(self.spread(53, self.slots8, self.near))
            self.advance(7, 5, 4, 3)
        elif name == "input":
            src = self.grad
            self.back(51 + n, src, n, tabs).start()
            self.keep(51 + n, src, n, tabs).start()
            if n == 0:
                total = self.gathered(53, self.slots8, self.near)
                self.slots4[0] = total
                self.start_all(self.spread(60, self.slots4, self.far))
            else:
                self.sm[...] = self.gathered(60, self.slots4, self.far)
        elif name == "leave":
            self.finish(tabs)

    def finish(self, tabs):
        self.y2_done()
        left = [c for c in range(len(self.state)) if self.state[c] < 5]
        while left:
            left.sort(key=lambda c: -self.state[c])
            self.advance(*left)
            left = [c for c in range(len(self.state)) if self.state[c] < 5]
        self.x2_done()
        fold = lambda values: sum(
            (values * values)[:, i * 128 : (i + 1) * 128] for i in range(values.shape[1] // 128)
        )
        tile = lambda rows: jnp.sum(rows.reshape(rows.shape[0] // 8, 8, 128), axis=0)
        square = tile(fold(self.final2[...]))
        for chunk in range(len(self.state)):
            square = square + tile(fold(self.final[chunk]))
        ends = [(self.final2, self.outs[2]), (self.final, self.outs[3]), (self.sm, self.outs[4])]
        ends = [pltpu.make_async_copy(src, dst, self.own_sem.at[3 + i]) for i, (src, dst) in enumerate(ends)]
        self.start_all(ends)
        self.square8[0] = square
        self.start_all(self.spread(64, self.square8, self.near))
        self.square4[0] = self.gathered(64, self.square8, self.near)
        self.start_all(self.spread(71, self.square4, self.far))
        small = tile(fold(self.sm[...]))
        whole = self.gathered(71, self.square4, self.far) + small
        end = pltpu.make_async_copy(self.square8.at[0], self.outs[5], self.own_sem.at[6])
        for chunk in range(len(self.state)):
            self.held[chunk] = ["w", "z", "y"]
            for number in range(5):
                self.phase(chunk, number).wait_send()
                name = self.order[chunk][number]
                if name in self.held[chunk]:
                    self.held[chunk].remove(name)
        sent = [self.core2(j) for j in range(4)] + [self.copy_z2(y) for y in range(2)]
        sent += [self.copy_w2(y) for y in range(2)] + [self.copy_y2(), self.copy_x2()]
        sent += [self.back(50, self.lo_h, 0, tabs)]
        sent += [self.back(51 + t, self.grad, t, tabs) for t in range(tabs)]
        sent += self.spread(53, self.slots8, self.near) + self.spread(60, self.slots4, self.far)
        for each in sent:
            each.wait_send()
        for each in self.spread(64, self.square8, self.near) + self.spread(71, self.square4, self.far):
            each.wait_send()
        self.square8[0] = whole
        end.start()
        self.back(50, self.lo_h, 0, tabs).wait_recv()
        self.keep(50, self.lo_h, 0, tabs).wait()
        for t in range(tabs):
            self.back(51 + t, self.grad, t, tabs).wait_recv()
            self.keep(51 + t, self.grad, t, tabs).wait()
        for each in ends:
            each.wait()
        end.wait()


def backward_kernel(
    count, a_h, g_h, dr2_h, h1_h, xh_h, rstd_h, rinv_h, ctx_h, q_h, k_h, v_h, x_h, e_h, lo_h,
    wqkv_h, wo_h, w1_h, w2_h, small_h, sg_h,
    *rest,
):
    outs, rest = rest[:count], rest[count:]
    A, U, W, WO, dr, df, h1, rstd, ctx, e, small, sm, g2, g1 = rest[:14]
    in_sem, e_sem, out_sem = rest[14:17]
    chunks, rows, width = A.shape
    tabs, pairs, length, _ = e_h.shape
    share = g1.shape[-2]
    corner = (slice(None),) * (len(U.shape) - 3) + (slice(0, share),)
    copy = pltpu.make_async_copy
    link = Link(rest[17:], g2, g1, U, sm, h1, lo_h, outs) if len(rest) > 17 else None
    loads = {}
    used = [0]

    def load(name, *both):
        loads[name] = []
        for src, dst in both:
            loads[name].append(copy(src, dst, in_sem.at[used[0]]))
            used[0] += 1
            loads[name][-1].start()

    def need(*names):
        for name in names:
            for loaded in loads[name]:
                loaded.wait()

    load("dr2", (dr2_h, dr))
    load("a", *[(a_h.at[j], A.at[j]) for j in range(chunks)])
    load("small", (small_h, small), (sg_h, sm.at[pl.ds(0, 8)]))
    load("w2", (w2_h, W))
    load("g", *[(g_h.at[j], U.at[j]) for j in range(chunks)])
    load("h1", (h1_h, h1))
    load("rstd", (rstd_h, rstd))
    load("wo", (wo_h, WO))
    load("ctx", (ctx_h, ctx))
    at = link.at if link else (lambda *key: None)
    at("enter")
    half = rows // 2
    halves = [slice(i * half, (i + 1) * half) for i in range(2)]
    inside = U.shape[2:]
    take = lambda j, i: U[j, i].reshape(half, width)
    need("small", "dr2")
    first = sm[0:8, :]
    blank = jnp.zeros((1, width), F32)
    order = [blank, first[0:1], blank, first[1:2], blank, blank, blank, first[2:3]]
    sm[...] = jnp.concatenate(order + [jnp.zeros((8, width), F32)], axis=0)
    gain1 = small_row(small, 0, width)
    df[...] = dr[...].astype(BF)

    for j in range(chunks):
        loads["a"][j].wait()
        g2[j] = tn(A[j], df[...]).astype(BF).reshape(g2.shape[1:])
        at("outer", j)
    load("qkv", *[(src, A.at[i]) for i, src in enumerate((q_h, k_h, v_h))])
    load("unit", (xh_h, A.at[3]))

    need("w2")
    for j in range(chunks):
        loads["g"][j].wait()
        total = blank
        for i, half_rows in enumerate(halves):
            d_active = nt(df[half_rows, :], W[j * width : (j + 1) * width, :])
            d_inner = (d_active * take(j, i).astype(F32)).astype(BF)
            U[j, i] = d_inner.reshape(inside)
            total = total + column_sum(d_inner.astype(F32))
        sm[8 + j : 9 + j, :] = total
        at("slope", j)
    load("w1", *[(w1_h.at[:, pl.ds(j * width, width)], W.at[pl.ds(j * width, width)]) for j in range(chunks)])

    need("h1")
    for j in range(chunks):
        g1[j] = tn(h1[...], U[j].reshape(rows, width)).astype(BF).reshape(g1.shape[1:])
        at("inner", j)

    load("rinv", (rinv_h, h1))
    need("w1", "rstd", "unit")
    d_gain, d_shift, d_bias = blank, blank, blank
    for i, half_rows in enumerate(halves):
        d_normed = dr[half_rows, :]
        for j in range(chunks):
            d_normed = d_normed + nt(take(j, i), W[j * width : (j + 1) * width, :])
        unit = A[3, half_rows, :].astype(F32)
        d_shift = d_shift + column_sum(d_normed)
        d_gain = d_gain + column_sum(d_normed * unit)
        d_unit = d_normed * gain1
        d_sum1 = d_unit - row_mean(d_unit) - unit * row_mean(d_unit * unit)
        d_sum1 = rstd[half_rows, 0:1] * d_sum1
        dr[half_rows, :] = d_sum1
        d_attn = d_sum1.astype(BF)
        df[half_rows, :] = d_attn
        d_bias = d_bias + column_sum(d_attn.astype(F32))
        at("norm", i)
    load("wqkv", (wqkv_h, W.at[pl.ds(0, 3 * width)]))
    load("x", (x_h, A.at[3]))
    sm[0:1, :] = d_gain
    sm[2:3, :] = d_shift
    sm[6:7, :] = d_bias

    need("ctx", "wo")
    U[(3,) + corner] = tn(ctx[...], df[...]).astype(BF).reshape(g1.shape[1:])
    at("attn")
    need("rinv")
    for half_rows in halves:
        d_ctx = nt(df[half_rows, :], WO[...]) * h1[half_rows, :].astype(F32)
        df[half_rows, :] = d_ctx.astype(BF)
    at("context")

    need("qkv", "x")
    masks = head_masks()
    zero = jnp.zeros((), BF)
    groups = 3
    wide = width // groups
    per_table = wide // (2 * HD)
    per_group = tabs * per_table
    steps = groups * per_group

    def place(n):
        table = lax.rem(n, per_group) // per_table
        return table, (n // per_group) * per_table + lax.rem(n, per_table)

    def fetch(n, slot):
        table, hp = place(n)
        copy(e_h.at[table, hp], e.at[slot], e_sem.at[slot]).start()

    fetch(0, 0)

    def attend(n, carry):
        table, hp = place(n)
        slot = lax.rem(n, 2)

        @pl.when(n + 1 < steps)
        def _():
            fetch(n + 1, 1 - slot)

        lanes = pl.ds(pl.multiple_of(hp * 2 * HD, 2 * HD), 2 * HD)
        here = pl.ds(pl.multiple_of(table * length, length), length)
        q2, k2, v2 = (A[i, here, lanes] for i in range(3))
        d_ctx = df[here, lanes]
        less = (-(ctx[here, lanes].astype(F32) * d_ctx.astype(F32))).astype(BF)
        right = jnp.concatenate([v2, jnp.ones((length, 2 * HD), BF)], axis=1)
        copy(e_h.at[0, 0], e.at[slot], e_sem.at[slot]).wait()
        d_query = d_key = d_value = None
        for h in range(2):
            mine = lambda values: jnp.where(masks[h], values, zero)
            d_head = mine(d_ctx)
            weights = e[slot, :, h * length : (h + 1) * length]
            d_raw = nt(jnp.concatenate([d_head, mine(less)], axis=1), right)
            d_scores = (weights.astype(F32) * d_raw).astype(BF)
            add = lambda held, new: new if held is None else held + new
            d_value = add(d_value, tn(weights, d_head))
            d_key = add(d_key, tn(d_scores, mine(q2)))
            d_query = add(d_query, nn(d_scores, mine(k2)))
        d_query = (d_query * (HD**-0.5)).astype(BF)
        d_value = d_value.astype(BF)
        A[0, here, lanes] = d_query
        A[1, here, lanes] = d_key.astype(BF)
        A[2, here, lanes] = d_value
        sm[4:5, lanes] = sm[4:5, lanes] + column_sum(d_query.astype(F32))
        sm[5:6, lanes] = sm[5:6, lanes] + column_sum(d_value.astype(F32))

        @pl.when(lax.rem(n, per_group) == per_group - 1)
        def _():
            g = n // per_group
            cols = pl.ds(pl.multiple_of(g * wide, wide), wide)
            grads = jnp.concatenate([A[i, :, cols] for i in range(3)], axis=1)
            U[(g,) + corner] = tn(A[3], grads).astype(BF).reshape(g1.shape[1:])

        at("attend", n)
        return carry

    lax.fori_loop(0, steps, attend, 0)
    at("attended")
    need("wqkv")
    for i, half_rows in enumerate(halves):
        d_input = dr[half_rows, :]
        for j in range(3):
            d_input = d_input + nt(A[j, half_rows, :], W[j * width : (j + 1) * width, :])
        h1[half_rows, :] = d_input.astype(BF)
        at("input", i)
    if link:
        at("leave")
        return
    pieces = [(h1, outs[0]), (g2, outs[1]), (g1, outs[2]), (U.at[3, :, pl.ds(0, share)], outs[3]), (sm, outs[4])]
    pieces += [(U.at[i, :, pl.ds(0, share)], outs[5].at[i]) for i in range(3)]
    ends = [copy(src, dst, out_sem.at[i]) for i, (src, dst) in enumerate(pieces)]
    for end in ends:
        end.start()
    for end in ends:
        end.wait()


def backward(saved, weights, small, mesh_bits):
    (x, q, k, v, e, rinv, ctx, h1, xh, rstd, a, g, dr2, lo, sg) = saved
    wqkv, wo, w1, w2 = weights
    chunks, rows, width = a.shape
    hidden = w1.shape[1]
    tabs, length = x.shape[:2]
    shape = jax.ShapeDtypeStruct
    linked = mesh_bits == (4, 1) and width % 256 == 0 and chunks == 4
    lead = (2, 2, 2, 2) if linked else (2,)
    share, part = width // math.prod(lead), rows // math.prod(lead)
    flat = lambda array: array.reshape(rows, array.shape[-1])
    g2 = shape((chunks, 2, 2, width // 4, width) if linked else (chunks, width, width), BF)
    g1 = shape((chunks,) + lead + (share, width), BF)
    go = shape(lead + (share, width), BF)
    small_sum = shape((16, width), F32)
    ins = (a, g.reshape((chunks,) + lead + (part, width)))
    ins += tuple(flat(array) for array in (dr2, h1, xh, rstd, rinv, ctx, q, k, v, x))
    ins += (e, lo, wqkv.reshape(3 * width, width), wo, w1, w2, small, sg)
    mem, dma = pltpu.VMEM, pltpu.SemaphoreType.DMA
    act = mem((rows, width), BF)
    scratch = [mem(a.shape, BF), mem(ins[1].shape, BF), mem(w2.shape, BF), mem(wo.shape, BF)]
    scratch += [mem((rows, width), F32), act, act, mem((rows, 128), F32), act]
    scratch += [mem((2,) + e.shape[2:], BF), mem(small.shape, F32), mem(small_sum.shape, F32)]
    scratch += [mem(array.shape, BF) for array in (g2, g1)]
    scratch += [dma((32,)), dma((2,)), dma((8,))]
    if linked:
        blocks = shape((2 * tabs, length // 2, width), BF)
        quarter, count, half = width // 4, chunks + 4, share // 2
        outs = [blocks, blocks, shape((quarter // 2, width), F32), shape((count, half, width), F32)]
        outs += [small_sum, shape((8, 128), F32)]
        scratch += [mem((2, 2, 2, quarter, width), BF), mem((2, 2, quarter, width), BF)]
        scratch += [mem((2, quarter, width), BF), mem((quarter, width), BF), mem((quarter // 2, width), BF)]
        scratch += [mem((count,) + (2,) * i + (share, width), BF) for i in (3, 2, 1, 0)]
        scratch += [mem((count, 32, width), BF)] * 2
        scratch += [mem(outs[2].shape, F32), mem(outs[3].shape, F32)]
        scratch += [mem((8,) + small_sum.shape, F32), mem((4,) + small_sum.shape, F32)]
        scratch += [mem((8, 8, 128), F32), mem((4, 8, 128), F32)]
        scratch += [dma((80,)), dma((80,)), dma((8,))]
        params = pltpu.CompilerParams(
            vmem_limit_bytes=VMEM_BYTES, collective_id=1, has_side_effects=True
        )
    else:
        outs = [shape((rows, width), BF), g2, g1, go, small_sum, shape((3,) + go.shape, BF)]
        params = pltpu.CompilerParams(vmem_limit_bytes=VMEM_BYTES)
    return linked, pl.pallas_call(
        functools.partial(backward_kernel, len(outs)),
        out_shape=outs,
        in_specs=anywhere(len(ins)),
        out_specs=anywhere(len(outs)),
        scratch_shapes=scratch,
        compiler_params=params,
        name="layer_backward",
    )(*ins)


def adam_update(grad_new, first, second, master, ema_old, rate):
    first_new = BETA_ONE * first + (1.0 - BETA_ONE) * grad_new
    second_new = BETA_TWO * second + (1.0 - BETA_TWO) * grad_new * grad_new
    fix_one = 1.0 - BETA_ONE**STEP
    fix_two = 1.0 - BETA_TWO**STEP
    master_new = master - rate * (
        first_new / fix_one / (jnp.sqrt(second_new / fix_two) + ADAM_EPS) + DECAY * master
    )
    ema_new = EMA_KEEP * ema_old + (1.0 - EMA_KEEP) * master_new
    return (first_new, second_new, master_new, ema_new)


def update_kernel(rates, clip_limit, names, *refs):
    total_in, outer_in, final_in, sum_in = refs[:4]
    states_in = [refs[4 + 4 * i : 8 + 4 * i] for i in range(5)]
    count_out = 6 * 4 + 5 + 1
    outs = refs[24 : 24 + count_out]
    refs = refs[24 + count_out :]
    total, outer, final, sums = refs[:4]
    states = [refs[4 + 4 * i : 8 + 4 * i] for i in range(5)]
    held = refs[24 : 24 + count_out]
    in_sem, out_sem = refs[24 + count_out :]
    copy = pltpu.make_async_copy
    loads = []

    def load(src, dst):
        loads.append(copy(src, dst, in_sem.at[len(loads)]))
        loads[-1].start()

    for src, dst in zip((total_in, outer_in, final_in, sum_in), (total, outer, final, sums)):
        load(src, dst)
    for group in range(5):
        for src, dst in zip(states_in[group], states[group]):
            load(src, dst)
    ends = []

    def end(index):
        ends.append(copy(held[index], outs[index], out_sem.at[index]))
        ends[-1].start()

    width = outer.shape[-1]
    for i in range(4):
        loads[i].wait()
    norm = jnp.sqrt(jnp.sum(jnp.sum(total[...], axis=0, keepdims=True), axis=1, keepdims=True))
    scale = jnp.minimum(1.0, clip_limit / norm)
    held[29][...] = norm
    end(29)
    third = width // 3
    for group in range(5):
        for i in range(4):
            loads[4 + 4 * group + i].wait()
        state = states[group]
        base = 6 * group
        kinds = held[base : base + (5 if group == 4 else 6)]
        if group == 0:
            spots = [(outer[...], (slice(None),))]
        elif group == 1:
            spots = [(final[j], (slice(None), slice(j * width, (j + 1) * width))) for j in range(4)]
        elif group == 2:
            spots = [(final[4], (slice(None),))]
        elif group == 3:
            spots = [
                (final[5 + j][:, i * third : (i + 1) * third], (i, slice(None), slice(j * third, (j + 1) * third)))
                for i in range(3)
                for j in range(3)
            ]
        else:
            lines = width // 128
            packed = [
                sums[r : r + 1, i * 128 : (i + 1) * 128]
                for r in range(kinds[0].shape[0] // lines)
                for i in range(lines)
            ]
            spots = [(jnp.concatenate(packed, axis=0), (slice(None),))]
        for summed, spot in spots:
            grad = summed * scale
            first, second, master, ema = adam_update(
                grad, state[1][spot], state[2][spot], state[0][spot], state[3][spot], rates[group]
            )
            if group == 4:
                results = (grad, first, second, master, ema)
            else:
                results = (grad, first, second, master, master.astype(BF), ema)
            for kind, result in zip(kinds, results):
                kind[spot] = result
        for i in range(len(kinds)):
            end(base + i)
    for each in ends:
        each.wait()


def update(total, outer, final, sums, states, rates, clip_limit):
    shape = jax.ShapeDtypeStruct
    outs = []
    for master, *_ in states[:4]:
        kind = shape(master.shape, F32)
        outs += [kind, kind, kind, kind, shape(master.shape, BF), kind]
    outs += [shape(states[4][0].shape, F32)] * 5 + [shape((1, 1), F32)]
    ins = (total, outer, final, sums) + tuple(array for group in states for array in group)
    mem, dma = pltpu.VMEM, pltpu.SemaphoreType.DMA
    return pl.pallas_call(
        functools.partial(update_kernel, rates, clip_limit, None),
        out_shape=outs,
        in_specs=anywhere(len(ins)),
        out_specs=anywhere(len(outs)),
        scratch_shapes=[mem(array.shape, array.dtype) for array in ins + tuple(outs)]
        + [dma((len(ins),)), dma((len(outs),))],
        compiler_params=pltpu.CompilerParams(vmem_limit_bytes=VMEM_BYTES),
        name="update",
    )(*ins)


def partner_swap(values, bit):
    count = lax.axis_size(AXES)
    return lax.ppermute(values, AXES, [(place, place ^ (1 << bit)) for place in range(count)])


def bit_order():
    bits = lax.axis_size(AXES).bit_length() - 1
    return list(range(1, bits)) + [0]


def scatter_sum(rows):
    order = bit_order()
    place = lax.axis_index(AXES)
    left = list(reversed(range(len(order))))
    held = rows.reshape((2,) * len(order) + rows.shape[1:])
    for bit in order:
        axis = left.index(bit)
        mine = (place >> bit) & 1
        keep = lax.dynamic_index_in_dim(held, mine, axis, keepdims=False)
        send = lax.dynamic_index_in_dim(held, 1 - mine, axis, keepdims=False)
        total = keep.astype(F32) + partner_swap(send, bit).astype(F32)
        left.remove(bit)
        held = total.astype(BF) if left else total
    return held


def butterfly_sum(values):
    for bit in bit_order():
        values = values + partner_swap(values, bit)
    return values


def sums_by_permutes(outs, width, tabs):
    grad, g2, g1, go, sums, gq = outs
    shards = lax.axis_size(AXES)
    outer = scatter_sum(g2.reshape(shards, -1)).reshape(-1, width)
    pieces = [g1.reshape(-1, shards, width // shards, width), go.reshape(1, shards, -1, width)]
    pieces = jnp.concatenate(pieces + [gq.reshape(-1, shards, width // shards, width)], axis=0)
    pieces = pieces.swapaxes(0, 1)
    final = scatter_sum(pieces.reshape(shards, -1)).reshape(pieces.shape[1:])
    sums = butterfly_sum(sums)
    total = butterfly_sum((jnp.sum(outer * outer) + jnp.sum(final * final)).reshape(1))
    total = jnp.zeros((8, 128), F32).at[0, 0].set(total[0] + jnp.sum(sums * sums))
    return grad, total, outer, final, sums


def unswap(rows, length):
    blocks = rows.reshape(-1, length, rows.shape[-1])
    return lax.all_to_all(blocks, "seq", split_axis=1, concat_axis=0, tiled=True)


def body(
    tables_in, out_cot, segment_ids, row_ids, col_ids,
    qkv_weight, out_weight, ffn_in_weight, ffn_out_weight, small_params,
    qkv_master, qkv_first, qkv_second, qkv_ema,
    out_master, out_first, out_second, out_ema,
    ffn_in_master, ffn_in_first, ffn_in_second, ffn_in_ema,
    ffn_out_master, ffn_out_first, ffn_out_second, ffn_out_ema,
    small_first, small_second, small_ema,
):
    width, hidden = ffn_in_weight.shape
    pack = lambda values: values.reshape(-1, 128)
    small = pack(small_params)
    weights = (qkv_weight, out_weight, ffn_in_weight, ffn_out_weight)
    saved = forward(tables_in, out_cot, segment_ids, row_ids, col_ids, *weights, small)
    bits = tuple(lax.axis_size(axis).bit_length() - 1 for axis in AXES)
    linked, outs = backward(saved, weights, small, bits)
    if linked:
        input_grad, layer_out, outer, final, sums, total = outs
    else:
        length = 2 * tables_in.shape[1]
        grad, total, outer, final, sums = sums_by_permutes(outs, width, tables_in.shape[0])
        input_grad, layer_out = unswap(grad, length), unswap(saved[13], length)
    states = [
        (ffn_out_master, ffn_out_first, ffn_out_second, ffn_out_ema),
        (ffn_in_master, ffn_in_first, ffn_in_second, ffn_in_ema),
        (out_master, out_first, out_second, out_ema),
        (qkv_master, qkv_first, qkv_second, qkv_ema),
        (small, pack(small_first), pack(small_second), pack(small_ema)),
    ]
    rates = (hidden**-0.5, width**-0.5, max(width // 128, 1) ** -0.5, width**-0.5, SMALL_RATE)
    entries = 4 * width * width + 2 * width * hidden + 8 * width + hidden
    new = update(total, outer, final, sums, states, rates, math.sqrt(float(entries)))
    wo_new, wi_new, o_new, qkv_new = (new[6 * i : 6 * i + 6] for i in range(4))
    sm_new = [values.reshape(-1) for values in new[24:29]]
    groups = (qkv_new, o_new, wi_new, wo_new)
    return (
        layer_out,
        input_grad,
        *[group[0] for group in groups],
        sm_new[0],
        new[29].reshape(()),
        *[values for group in groups for values in group[1:]],
        sm_new[1],
        sm_new[2],
        sm_new[3],
        sm_new[4],
    )


def solution(mesh):
    rows = P("batch", "seq", None)
    ids = P("batch", None)
    shard3 = P(None, AXES, None)
    shard2 = P(AXES, None)
    in_specs = (rows, rows, ids, ids, ids) + (P(),) * 5 + (shard3,) * 4 + (shard2,) * 12 + (P(),) * 3
    out_specs = (rows, rows, shard3, shard2, shard2, shard2, P(), P())
    out_specs += (shard3,) * 5 + (shard2,) * 15 + (P(),) * 4
    return jax.shard_map(body, mesh=mesh, in_specs=in_specs, out_specs=out_specs, check_vma=False)
```

time: 611 us -> 208 us (0.34); the launches traced: 599 us -> 204 us
  Pallas kernels: 0 us -> 200 us
  matrix products: 186 us -> 0 us
  waiting for transfers between devices: 134 us -> 0 us
  local copies, waits for them, and re-layouts: 131 us -> 3.11 us
  other arithmetic: 85.8 us -> 0 us
  starting transfers between devices: 53.2 us -> 0 us
  between operations: 9.71 us -> 0.99 us
    pallas_call x0 -> x3, Pallas kernels: none -> 200 us  [the longest x1 136 us: backward(): pl.pallas_call(functools.partial(backward_kernel, len(outs)), out_shape=o...]
    dot_general x24 -> x0, matrix products: 186 us -> none  [the longest x6 53.8 us: product(): return jnp.dot(left, right, preferred_element_type=jnp.float32)]
    ppermute x30 -> x0, waiting for transfers between devices: 100 us -> none  [partner_swap(): lax.ppermute(values, AXES, [(place, place ^ 1 << bit) for place in range(...]
    convert_element_type x14 -> x0, local copies, waits for them, and re-layouts: 64.2 us -> none  [the longest x5 44 us: scatter_sum(): held = rows.astype(jnp.bfloat16).reshape((2,) * len(order) + rows.shape[1:])]
    convert_element_type x22 -> x0, other arithmetic: 47.2 us -> none  [the longest x1 21.9 us: body(): d_scores_low = d_scores.astype(jnp.bfloat16)]
    ppermute x30 -> x0, starting transfers between devices: 35.5 us -> none  [partner_swap(): lax.ppermute(values, AXES, [(place, place ^ 1 << bit) for place in range(...]
    all_to_all x4 -> x0, waiting for transfers between devices: 33.8 us -> none  [the longest x2 18.7 us: body(): lax.all_to_all(rows, 'seq', split_axis=0, concat_axis=1, tiled=True)]
    reduce_sum x14 -> x0, other arithmetic: 25.5 us -> none  [the longest x1 11.1 us: body(): exp_total = jnp.sum(exp_scores, axis=-1, keepdims=True)]
  transfers between devices with their start and end apart: 34 -> 0, of which waited for: 17 -> 0; matrix products, arithmetic and copies ran while one was open for 27% -> 0% of each run, Pallas kernels for 0% -> 0%
where the time goes in v2:
time: 208 us; the launch traced here: 204 us
  Pallas kernels  200 us (96%)
  local copies, waits for them, and re-layouts  3.11 us (1%)
    pallas_call x1, Pallas kernels, backward(): pl.pallas_call(functools.partial(backward_kernel, len(outs)), out_shape=o...  136 us
    pallas_call x1, Pallas kernels, forward(): pl.pallas_call(forward_kernel, out_shape=outs, in_specs=anywhere(len(ins)...  59.9 us
    pallas_call x1, Pallas kernels, update(): pl.pallas_call(functools.partial(update_kernel, rates, clip_limit, None),...  4.51 us

profile of v2, /device:TPU:0, one launch (start us, length us, event | category | flops | bytes accessed | tf_op | source)
XLA Modules:
  0.0 204.3 jit_solution(5388180226064614491)
XLA Ops:
  0.7 59.9 %layer_forward.1 = (bf16[2,512,768]{2,1,0:T(8,128)(2,1)}, bf16[2,512,768]{2,1,0:T(8,128)(2,1)}, bf16[2,512,768]{2,1,0:T(8,128)(2,1)}, bf16[2,512,768]{2,1,0:T(8,...) custom-call(bf16[4,256,768]{2,1,0:T(8,128)(2,1)} %tables_h.1, ...), custom_call_target="tpu_custom_call" | custom-call | tf_op jit(solution)/shard_map/layer_forward/pallas_call | solution.py:257
  60.6 135.8 %layer_backward.1 = (bf16[4,256,768]{2,1,0:T(8,128)(2,1)}, bf16[4,256,768]{2,1,0:T(8,128)(2,1)}, f32[96,768]{1,0:T(8,128)}, f32[8,24,768]{2,1,0:T(8,128)}, f32[16,768]{1,0:T(8,128)}, /*index=5*/f32[8,128]{1,0:T(8,128)}) custom-call(bf16[4,1024,768]{2,1,0:T(8,128)(2,1)} %get-tuple-element.83.a_h, bf16[4,2,2,2,2,64,768]{6,5,4,3,2,1,0:T(8,128)(2,1)} %bitcast.23, ...), custom_call_target="tpu_custom_call" | custom-call | tf_op jit(solution)/shard_map/layer_backward/pallas_call | solution.py:826
  196.4 0.0 copy-start.1
  196.4 4.5 %update.1 = (f32[96,768]{1,0:T(8,128)}, f32[96,768]{1,0:T(8,128)}, f32[96,768]{1,0:T(8,128)}, f32[96,768]{1,0:T(8,128)}, bf16[96,768]{1,0:T(8,128)(2,1)}, /*inde...) custom-call(f32[8,128]{1,0:T(8,128)} %get-tuple-element.100.refs_0_,, ...), custom_call_target="tpu_custom_call" | custom-call | tf_op jit(solution)/shard_map/update/pallas_call | solution.py:937
  200.9 0.0 copy-done.1
  200.9 0.0 copy-start
  200.9 1.1 copy.63
  202.1 0.8 copy-done
  202.9 1.1 copy.64
Async XLA Ops:
  196.4 4.5 %copy-start.1 = (bf16[4,256,768]{2,1,0:T(8,128)(2,1)S(1)}, bf16[4,256,768]{2,1,0:T(8,128)(2,1)}, u32[]{:S(2)}) copy-start(bf16[4,256,768]{2,1,0:T(8,128)(2,1)} %get-tuple-element.166) | copy-start | bytes 4718596
  200.9 2.0 copy-start
